TPU v7x, 512 devices: a whole 4x8x8 slice. The times are simulated.
512 devices in a mesh: fsdp: 64 (over x, y, core), replica: 8 (over z).
Axes of the slice: x: 4, y: 8, z: 8, core: 2. Of those that a mesh axis runs over, the one named last changes fastest.
Arguments:
- gradient: bfloat16 [16, 1024, 8, 1024], P(None, 'fsdp', None, 'replica')
- second_moment: bfloat16 [16, 1024, 8, 1024], P(None, 'fsdp', None, 'replica'), may hold values from 0.25 to 4
- momentum: bfloat16 [16, 1024, 8, 1024], P(None, 'fsdp', None, 'replica'), may hold values from -3 to 3
- left_factor: bfloat16 [192, 1024, 1024], P('fsdp', 'replica')
- right_factor: bfloat16 [192, 1024, 1024], P('fsdp', None, 'replica')
- block_of_slot: int32 [64, 3], replicated, may hold values from -1 to 127, as said below
Outputs:
- momentum_new: bfloat16 [16, 1024, 8, 1024], P(None, 'fsdp', None, 'replica')
- moment_new: bfloat16 [16, 1024, 8, 1024], P(None, 'fsdp', None, 'replica')
Inputs may be any that keep to these rules, and one draw needn't show every extreme that they name: `block_of_slot`: every block appears in exactly one slot; an owner holds 0 to 3 blocks and at least one owner holds exactly 3; all other slots hold -1.
All inputs are finite; a program needn't handle non-finite values.
Results may differ from a plain program's by a relative error of at most 0.0057.
Values may be sent and summed in bfloat16 or wider, within the bound.
No kernel may reach another device: no remote copies, remote signals or barrier semaphores. Data moves between devices by JAX's collectives and lax.ppermute only.
A program may use at most 64 MiB of HBM per device.

v0:
```python
import jax
import jax.numpy as jnp
from jax import lax
from jax.sharding import PartitionSpec as P

BETA_ONE = 0.9
BETA_TWO = 0.999
ADAM_EPS = 1e-08
NORM_EPS = 1e-06


def adam_terms(gradient_f, second_f):
    moment_new = BETA_TWO * second_f + (1.0 - BETA_TWO) * gradient_f * gradient_f
    return (moment_new, gradient_f / (jnp.sqrt(moment_new) + ADAM_EPS))


def as_pieces(array, block_count):
    shard_rows = array.shape[1]
    shard_cols = array.shape[3]
    return jnp.transpose(array, (0, 2, 1, 3)).reshape(block_count, shard_rows, shard_cols)


def by_slot(values, slot_index, slot_live):
    chosen = jnp.take(values, slot_index, axis=0)
    return jnp.where(slot_live[:, None, None], chosen, jnp.zeros((), values.dtype))


def local(gradient, second_moment, momentum, left_factor, right_factor, block_of_slot):
    block_rows, shard_rows, block_cols, shard_cols = gradient.shape
    block_count = block_rows * block_cols
    slot_block = block_of_slot.reshape(-1)
    slot_live = slot_block >= 0
    slot_index = jnp.where(slot_live, slot_block, 0)
    owner_block = lax.dynamic_index_in_dim(block_of_slot, lax.axis_index("fsdp"), 0, keepdims=False)
    owner_live = owner_block >= 0
    owner_index = jnp.where(owner_live, owner_block, 0)
    moment_new, adam_step = adam_terms(
        gradient.astype(jnp.float32), second_moment.astype(jnp.float32)
    )
    block_pieces = by_slot(as_pieces(gradient, block_count), slot_index, slot_live)
    partial_value = jnp.sum(adam_step * adam_step, axis=(1, 3)).reshape(block_count)
    adam_totals = lax.psum(partial_value, ("fsdp", "replica"))
    owner_grad = lax.all_to_all(block_pieces, "fsdp", split_axis=0, concat_axis=1, tiled=True)
    left_done = jnp.einsum(
        "sij,sjk->sik",
        left_factor,
        lax.all_gather(owner_grad, "replica", axis=2, tiled=True),
        preferred_element_type=jnp.float32,
    ).astype(jnp.bfloat16)
    shampoo = jnp.einsum(
        "sij,sjk->sik",
        lax.all_gather(left_done, "replica", axis=1, tiled=True),
        right_factor,
        preferred_element_type=jnp.float32,
    )
    shampoo_square = jnp.sum(shampoo * shampoo, axis=(1, 2))
    shampoo_total = lax.psum(shampoo_square, "replica")
    adam_total = jnp.where(
        owner_live, jnp.take(adam_totals, owner_index), jnp.zeros((), jnp.float32)
    )
    graft_scale = jnp.sqrt(adam_total) / jnp.sqrt(shampoo_total + NORM_EPS)
    grafted = (shampoo * graft_scale[:, None, None]).astype(jnp.bfloat16)
    returned = lax.all_to_all(grafted, "fsdp", split_axis=1, concat_axis=0, tiled=True)
    slot_total = slot_block.shape[0]
    target = jnp.where(slot_live, slot_block, block_count)
    block_place = (
        jnp.zeros((block_count,), jnp.int32)
        .at[target]
        .set(jnp.arange(slot_total, dtype=jnp.int32), mode="drop")
    )
    placed = jnp.take(returned, block_place, axis=0)
    placed = jnp.transpose(
        placed.reshape(block_rows, block_cols, shard_rows, shard_cols), (0, 2, 1, 3)
    )
    momentum_new = BETA_ONE * momentum.astype(jnp.float32) + placed.astype(jnp.float32)
    return (momentum_new.astype(jnp.bfloat16), moment_new.astype(jnp.bfloat16))


def solution(mesh):
    in_specs = (
        P(None, "fsdp", None, "replica"),
        P(None, "fsdp", None, "replica"),
        P(None, "fsdp", None, "replica"),
        P("fsdp", "replica", None),
        P("fsdp", None, "replica"),
        P(),
    )
    out_specs = (P(None, "fsdp", None, "replica"), P(None, "fsdp", None, "replica"))
    return jax.shard_map(local, mesh=mesh, in_specs=in_specs, out_specs=out_specs, check_vma=False)
```

profile of v0, /device:TPU:1, one launch (start us, length us, event | category | flops | bytes accessed | tf_op | source)
XLA Modules:
  0.0 299.6 jit_solution(16030026426160500408)
XLA Ops:
  7.2 0.0 all-gather.3.cloned.1.call-start
  7.2 0.9 copy.25
  8.1 0.1 reshape.120
  8.3 0.1 reshape.121
  8.4 1.1 copy.27
  9.6 0.8 gather_fusion
  10.4 0.9 select_select_fusion
  11.3 34.4 %all_to_all.36 = bf16[192,16,128]{2,1,0:T(8,128)(2,1)S(1)} all-to-all(bf16[192,16,128]{2,1,0:T(8,128)(2,1)S(1)} %select_select_fusion), channel_id=1, replica_groups=mesh['fsdp'=64,'replica'=8] {'fsdp'}, dimensions={0} | all-to-all | bytes 1572864 | tf_op jit(solution)/shard_map/all_to_all | solution.py:43
  45.7 0.1 copy.28
  45.9 1.2 copy.29
  47.0 0.0 all-gather.3.cloned.1.call-update
  47.1 0.0 all-gather.5.cloned.1.call-start
  47.2 78.0 %all-gather.3.cloned.1.call-done = bf16[3,1024,1024]{1,2,0:T(8,128)(2,1)} async-done(((bf16[3,1024,128]{1,2,0:T(8,128)(2,1)}), bf16[3,1024,1024]{1,2,0:T(8,128)(2,1)}) %all-gather.3.cloned.1.call-update) | async-done | bytes 6291472 | tf_op jit(solution)/shard_map/all_gather | solution.py:47
  125.2 5.5 %fusion = bf16[3,128,1024]{1,2,0:T(8,128)(2,1)} fusion(bf16[3,1024,1024]{1,2,0:T(8,128)(2,1)} %all-gather.3.cloned.1.call-done, bf16[3,128,1024]{2,1,0:T(8,128)(2,1)S(1)} %copy-done.5), kind=kOutput, calls=%fused_computation.9 | convolution fusion | flops 805699584 | bytes 7864320 | tf_op jit(solution)/shard_map/sij,sjk->sik/dot_general | solution.py:44
  130.7 1.5 fusion.4
  132.2 0.1 reshape.123
  132.3 0.2 dynamic-slice_reduce_fusion
  132.5 98.6 %psum.14 = f32[128]{0:T(128)S(1)} all-reduce(f32[128]{0:T(128)S(1)} %reshape.123), channel_id=1, replica_groups=mesh['fsdp'=64,'replica'=8] {'fsdp','replica'}, use_global_device_ids=true, to_apply=%region_2.3 | all-reduce | flops 128 | bytes 1024 | tf_op jit(solution)/shard_map/psum | solution.py:42
  231.1 0.6 gather_fusion.1
  231.8 5.2 %multiply_reduce_fusion = (f32[3]{0:T(128)S(1)}, f32[3,1024,128]{2,1,0:T(8,128)S(1)}) fusion(bf16[3,1024,1024]{1,2,0:T(8,128)(2,1)} %all-gather.5.cloned.1.call-done, bf16[3,1024,128]{2,1,0:T(8,128)(2,1)S(1)} %copy-done), kind=kOutput, calls=%fused_computation.5 | convolution fusion | flops 806092800 | bytes 8650764 | tf_op jit(solution)/shard_map/sij,sjk->sik/dot_general | solution.py:50
  236.9 12.5 %psum.15 = f32[3]{0:T(128)S(1)} all-reduce(f32[3]{0:T(128)S(1)} %get-tuple-element.14), channel_id=1, replica_groups=mesh['fsdp'=64,'replica'=8] {'replica'}, use_global_device_ids=true, to_apply=%region_4.5 | all-reduce | flops 3 | bytes 24 | tf_op jit(solution)/shard_map/psum | solution.py:57
  249.5 0.2 multiply_convert_fusion
  249.7 1.7 copy.31
  251.3 10.6 %all-to-all-start.1 = ((bf16[3,1024,128]{2,0,1:T(4,128)(2,1)}), bf16[3,1024,128]{2,0,1:T(4,128)(2,1)S(1)}, u32[]{:S(2)}, u32[]{:S(2)}) async-start(bf16[3,1024,128]{2,0,1:T(4,128)(2,1)} %copy.31), calls=%async_computation.1 | async-start | bytes 2097152 | tf_op jit(solution)/shard_map/all_to_all | solution.py:63
  262.0 1.2 scatter_custom_fusion
  263.2 0.1 broadcast_in_dim.59
  263.3 27.2 %all-to-all-done.1 = bf16[3,1024,128]{2,0,1:T(4,128)(2,1)S(1)} async-done(((bf16[3,1024,128]{2,0,1:T(4,128)(2,1)}), bf16[3,1024,128]{2,0,1:T(4,128)(2,1)S(1)}, u32[]{:S(2)}, u32[]{:S(2)}) %all-to-all-start.1) | async-done | bytes 786464 | tf_op jit(solution)/shard_map/all_to_all | solution.py:63
  290.5 0.1 copy.32
  290.7 0.1 copy.33
  290.8 0.7 gather_fusion.2
  291.5 0.3 fusion.3
  291.8 0.9 copy.34
  (24 shorter events, 0.1 us)
Async XLA Ops:
  7.2 224.6 %copy-start = (bf16[3,1024,128]{2,1,0:T(8,128)(2,1)S(1)}, bf16[3,1024,128]{2,1,0:T(8,128)(2,1)}, u32[]{:S(2)}) copy-start(bf16[3,1024,128]{2,1,0:T(8,128)(2,1)} %param.10) | copy-start | bytes 2359300
  7.2 118.0 %copy-start.5 = (bf16[3,128,1024]{2,1,0:T(8,128)(2,1)S(1)}, bf16[3,128,1024]{2,1,0:T(8,128)(2,1)}, u32[]{:S(2)}) copy-start(bf16[3,128,1024]{2,1,0:T(8,128)(2,1)} %param.9) | copy-start | bytes 2359300
  7.2 118.0 %all-gather.3.cloned.1.call-start = ((), (), s32[]{:S(2)}) async-start(), calls=%async_computation.2 | async-start | bytes 7077888 | tf_op jit(solution)/shard_map/all_gather | solution.py:47
  47.1 83.6 %copy-start.1 = (bf16[16,16,8,128]{3,2,1,0:T(8,128)(2,1)S(1)}, bf16[16,16,8,128]{3,2,1,0:T(8,128)(2,1)}, u32[]{:S(2)}) copy-start(bf16[16,16,8,128]{3,2,1,0:T(8,128)(2,1)} %param.6) | copy-start | bytes 1572868
  47.1 83.6 %copy-start.2 = (bf16[16,16,8,128]{3,2,1,0:T(8,128)(2,1)S(1)}, bf16[16,16,8,128]{3,2,1,0:T(8,128)(2,1)}, u32[]{:S(2)}) copy-start(bf16[16,16,8,128]{3,2,1,0:T(8,128)(2,1)} %param.7) | copy-start | bytes 1572868
  47.1 85.2 %copy-start.4 = (s32[64,3]{0,1:T(4,128)S(1)}, s32[64,3]{0,1:T(4,128)}, u32[]{:S(2)}) copy-start(s32[64,3]{0,1:T(4,128)} %param.11) | copy-start | bytes 2308
  47.1 184.7 %all-gather.5.cloned.1.call-start = ((), (), s32[]{:S(2)}) async-start(), calls=%async_computation.3 | async-start | bytes 7077888 | tf_op jit(solution)/shard_map/all_gather | solution.py:52
  236.9 54.6 %copy-start.3 = (bf16[16,16,8,128]{3,2,1,0:T(8,128)(2,1)S(1)}, bf16[16,16,8,128]{3,2,1,0:T(8,128)(2,1)}, u32[]{:S(2)}) copy-start(bf16[16,16,8,128]{3,2,1,0:T(8,128)(2,1)} %param.8) | copy-start | bytes 1572868
  251.3 39.2 %all-to-all-start.1 = ((bf16[3,1024,128]{2,0,1:T(4,128)(2,1)}), bf16[3,1024,128]{2,0,1:T(4,128)(2,1)S(1)}, u32[]{:S(2)}, u32[]{:S(2)}) async-start(bf16[3,1024,128]{2,0,1:T(4,128)(2,1)} %copy.31), calls=%async_computation.1 | async-start | bytes 2097152 | tf_op jit(solution)/shard_map/all_to_all | solution.py:63
Sparse Core Ops, SparseCore 0:
  47.2 77.9 all-gather.2
  130.8 80.8 all-gather.4
where the time goes:
time: 300 us
  blocking collectives  145 us (48%)
  waiting for transfers between devices  105 us (35%)
  between operations  14.3 us (5%)
  starting transfers between devices  10.7 us (4%)
  matrix products  10.6 us (4%)
  local copies, waits for them, and re-layouts  10.2 us (3%)
  other arithmetic  3.03 us (1%)
    psum x1, blocking collectives, local(): adam_totals = lax.psum(partial_value, ('fsdp', 'replica'))  98.6 us
    all_gather x1, waiting for transfers between devices, local(): lax.all_gather(owner_grad, 'replica', axis=2, tiled=True)  78 us
    all_to_all x1, blocking collectives, local(): lax.all_to_all(block_pieces, 'fsdp', split_axis=0, concat_axis=1, tiled=T...  34.4 us
    all_to_all x1, waiting for transfers between devices, local(): lax.all_to_all(grafted, 'fsdp', split_axis=1, concat_axis=0, tiled=True)  27.2 us
    psum x1, blocking collectives, local(): shampoo_total = lax.psum(shampoo_square, 'replica')  12.5 us
    all_to_all x1, starting transfers between devices, local(): lax.all_to_all(grafted, 'fsdp', split_axis=1, concat_axis=0, tiled=True)  10.6 us
  transfers between devices with their start and end apart: 3, of which 2 were waited for; matrix products, arithmetic and copies ran while one was open for 1% of the time, Pallas kernels for 0%

commit v1 on v0

v1 whole, which is shorter than its diff:
```python
import jax
import jax.numpy as jnp
from jax import lax
from jax.experimental import pallas as pl
from jax.experimental.pallas import tpu as pltpu
from jax.sharding import Mesh
from jax.sharding import PartitionSpec as P

BETA_ONE = 0.9
BETA_TWO = 0.999
ADAM_EPS = 1e-08
NORM_EPS = 1e-06

COL = ("x1", "x0", "y2", "y1", "y0")
REPLICA = ("z2", "z1", "z0")
RING = 8
COLS = 32
SLOTS = 3
PLACES = 4
CORES = 2
NOTE = 3

ANY = pl.BlockSpec(memory_space=pl.ANY)
VMEM = pl.BlockSpec(memory_space=pltpu.VMEM)
SMEM = pl.BlockSpec(memory_space=pltpu.SMEM)


def limit(mebibytes):
    return pltpu.CompilerParams(vmem_limit_bytes=mebibytes * 1024 * 1024)


def high_low(value):
    high = value.astype(jnp.bfloat16).astype(jnp.float32)
    return high, value - high


def member(col, place):
    return col * RING + place


def factor_pairs(step):
    pairs = []
    for c in range(CORES):
        for s in range(SLOTS):
            root = PLACES * c + s
            near, far = (root + step) % RING, (root + step + PLACES) % RING
            if step > 0:
                pairs.append((c * RING + near, c * RING + root))
            pairs.append((c * RING + far, (1 - c) * RING + root))
    return pairs


def factor_kernel(left, right, *outs):
    part = left.shape[1]
    here = lax.axis_index(REPLICA)
    for step in range(PLACES):
        slot = lax.rem(here - step + RING, PLACES)

        @pl.when(slot < SLOTS)
        def _():
            for j in range(RING):
                outs[step][j] = left[slot, :, j * part : (j + 1) * part]
                outs[step][RING + j] = right[slot, j * part : (j + 1) * part, :]


def spread_factors(left, right):
    part = left.shape[1]
    return pl.pallas_call(
        factor_kernel,
        out_shape=[jax.ShapeDtypeStruct((2 * RING, part, part), left.dtype)] * PLACES,
        in_specs=[VMEM, VMEM],
        out_specs=[VMEM] * PLACES,
        compiler_params=limit(16),
        name="spread_factors",
    )(left, right)


def prepare_kernel(slots, gradient, second, after, moment, pieces, place, wide, square, notes):
    block_rows, shard_rows, block_cols, lanes = gradient.shape
    per_row = shard_rows * block_cols

    def adam(i, carry):
        g = gradient[i].astype(jnp.float32)
        v = BETA_TWO * second[i].astype(jnp.float32) + (1.0 - BETA_TWO) * g * g
        moment[i] = v.astype(moment.dtype)
        step = g / (jnp.sqrt(v) + ADAM_EPS)
        square[pl.ds(pl.multiple_of(i * block_cols, block_cols), block_cols), :] = jnp.sum(step * step, axis=0)
        wide[pl.ds(pl.multiple_of(i * per_row, per_row), per_row), :] = g.reshape(per_row, lanes)
        return carry

    lax.fori_loop(0, block_rows, adam, 0)
    notes[...] = jnp.zeros(notes.shape, notes.dtype)

    def column(col, carry):
        for c in range(CORES):
            for s in range(SLOTS):
                held = slots[col * CORES + c, s]
                block = jnp.maximum(held, 0)
                i = lax.div(block, block_cols)
                j = lax.rem(block, block_cols)
                piece = wide[pl.ds(i * per_row + j, shard_rows, stride=block_cols), :]
                pieces[member(col, PLACES * c + s)] = piece.astype(pieces.dtype)
                high, low = high_low(square[pl.ds(block, 1), :])
                row = 2 * (SLOTS * c + s)
                notes[row : row + 1, :] = high
                notes[row + 1 : row + 2, :] = low

                @pl.when(held >= 0)
                def _():
                    place[0, block] = member(col, PLACES * c + s)
                    place[1, block] = col * shard_rows + row

        pieces[member(col, NOTE)] = notes[...].astype(pieces.dtype)
        return carry

    lax.fori_loop(0, COLS, column, 0)


def prepare(slots, gradient, second, after):
    block_rows, shard_rows, block_cols, lanes = gradient.shape
    block_count = block_rows * block_cols
    return pl.pallas_call(
        prepare_kernel,
        out_shape=[
            jax.ShapeDtypeStruct(second.shape, second.dtype),
            jax.ShapeDtypeStruct((COLS * RING, shard_rows, lanes), gradient.dtype),
            jax.ShapeDtypeStruct((2, block_count), jnp.int32),
        ],
        in_specs=[SMEM, VMEM, VMEM, ANY],
        out_specs=[VMEM, VMEM, SMEM],
        scratch_shapes=[
            pltpu.VMEM((block_count * shard_rows, lanes), jnp.float32),
            pltpu.VMEM((block_count, lanes), jnp.float32),
            pltpu.VMEM((shard_rows, lanes), jnp.float32),
        ],
        compiler_params=limit(16),
        name="prepare",
    )(slots, gradient, second, after)


def together_kernel(columns, own, *refs):
    factors, out = refs[:PLACES], refs[PLACES]
    count = columns.shape[0]
    size = own.shape[0] * own.shape[1] // columns.shape[1]
    at_home = lax.div(lax.axis_index(REPLICA), PLACES) == lax.axis_index("core")
    out[:count] = columns[...]
    for step in range(1, PLACES):
        out[count + step * size : count + (step + 1) * size] = factors[step][...].reshape((size,) + columns.shape[1:])

    @pl.when(at_home)
    def _():
        out[count : count + size] = own[...].reshape((size,) + columns.shape[1:])

    @pl.when(jnp.logical_not(at_home))
    def _():
        out[count : count + size] = factors[0][...].reshape((size,) + columns.shape[1:])


def together(columns, own, factors):
    count, rows, part = columns.shape
    count += PLACES * own.shape[0] * own.shape[1] // rows
    return pl.pallas_call(
        together_kernel,
        out_shape=jax.ShapeDtypeStruct((count, rows, part), columns.dtype),
        in_specs=[VMEM] * (2 + PLACES),
        out_specs=VMEM,
        compiler_params=limit(16),
        name="together",
    )(columns, own, *factors)


def block_kernel(own, swapped, out, lf, rf, grad, half, full, notes):
    rows, part = own.shape[1:]
    order = lf.shape[0]
    count = COLS * RING
    groups = part // rows
    core = lax.axis_index("core")
    here = lax.axis_index(REPLICA)
    place = lax.rem(here, PLACES)

    @pl.when(place < SLOTS)
    def _():
        owner_core = lax.div(here, PLACES)
        for b, held in enumerate((own, swapped)):
            h = core if b == 0 else 1 - core
            for col in range(COLS):
                for r in range(RING):
                    grad[col, h, :, r * part : (r + 1) * part] = held[member(col, r)]
            for step in range(PLACES):
                source = lax.rem(here + step + jnp.where(h == owner_core, 0, PLACES), RING)
                at = pl.ds(pl.multiple_of(source * part, part), part)
                for j in range(RING):
                    left = count + (2 * RING * step + j) * groups
                    right = left + RING * groups
                    lf[at, j * part : (j + 1) * part] = held[left : left + groups].reshape(part, part)
                    rf[j * part : (j + 1) * part, at] = held[right : right + groups].reshape(part, part)

        tile = 2 * part
        steps = order // tile

        def first(t, carry):
            at = pl.ds(pl.multiple_of(t * tile, tile), tile)
            rhs = grad[:, :, :, at].reshape(order, tile)
            half[:, at] = jnp.dot(lf[...], rhs, preferred_element_type=jnp.float32).astype(half.dtype)
            return carry

        lax.fori_loop(0, steps, first, 0, unroll=True)

        def second(t, square):
            at = pl.ds(pl.multiple_of(t * tile, tile), tile)
            value = jnp.dot(half[...], rf[:, at], preferred_element_type=jnp.float32)
            full[:, :, :, at] = value.reshape(COLS, CORES, rows, tile)
            return square + jnp.sum(value * value, axis=0, keepdims=True)

        square = lax.fori_loop(0, steps, second, jnp.zeros((1, tile), jnp.float32), unroll=True)
        square = jnp.sum(square, axis=1, keepdims=True)
        scale = 1.0 / jnp.sqrt(square + NORM_EPS)
        for r in range(RING):
            value = (full[:, core, :, r * part : (r + 1) * part] * scale).astype(out.dtype)
            for col in range(COLS):
                out[member(col, r)] = value[col]

    @pl.when(place == NOTE)
    def _():
        total = jnp.zeros(notes.shape, jnp.float32)
        for held in (own, swapped):
            total = total + jnp.sum(held[:count].astype(jnp.float32), axis=0)
        notes[...] = total
        for row in range(0, 2 * CORES * SLOTS, 2):
            high, low = high_low(notes[row : row + 1, :] + notes[row + 1 : row + 2, :])
            notes[row : row + 1, :] = high
            notes[row + 1 : row + 2, :] = low
        out[...] = jnp.broadcast_to(notes[...].astype(out.dtype), out.shape)


def precondition(own, swapped):
    _, rows, part = own.shape
    order = RING * part
    kind = own.dtype
    return pl.pallas_call(
        block_kernel,
        out_shape=jax.ShapeDtypeStruct((COLS * RING, rows, part), kind),
        in_specs=[VMEM] * 2,
        out_specs=VMEM,
        scratch_shapes=[
            pltpu.VMEM((order, order), kind),
            pltpu.VMEM((order, order), kind),
            pltpu.VMEM((COLS, CORES, rows, order), kind),
            pltpu.VMEM((order, order), kind),
            pltpu.VMEM((COLS, CORES, rows, order), jnp.float32),
            pltpu.VMEM((rows, part), jnp.float32),
        ],
        compiler_params=limit(28),
        cost_estimate=pl.CostEstimate(flops=4 * order**3, bytes_accessed=10 * order * order, transcendentals=0),
        name="precondition",
    )(own, swapped)


def finish_kernel(place, returned, momentum, out, wide, adam):
    block_rows, shard_rows, block_cols, lanes = momentum.shape
    for col in range(COLS):
        note = jnp.sum(returned[member(col, NOTE)].astype(jnp.float32), axis=1, keepdims=True)
        adam[col * shard_rows : (col + 1) * shard_rows, :] = jnp.broadcast_to(note, (shard_rows, lanes))

    def step(i, carry):
        for j in range(block_cols):
            block = i * block_cols + j
            row = place[1, block]
            scale = jnp.sqrt(adam[pl.ds(row, 1), :] + adam[pl.ds(row + 1, 1), :])
            piece = returned[place[0, block]].astype(jnp.float32) * scale
            wide[pl.ds(j, shard_rows, stride=block_cols), :] = piece
        grafted = wide[...].reshape(shard_rows, block_cols, lanes)
        out[i] = (BETA_ONE * momentum[i].astype(jnp.float32) + grafted).astype(out.dtype)
        return carry

    lax.fori_loop(0, block_rows, step, 0)


def finish(place, returned, momentum):
    block_rows, shard_rows, block_cols, lanes = momentum.shape
    return pl.pallas_call(
        finish_kernel,
        out_shape=jax.ShapeDtypeStruct(momentum.shape, momentum.dtype),
        in_specs=[SMEM, VMEM, VMEM],
        out_specs=VMEM,
        scratch_shapes=[
            pltpu.VMEM((shard_rows * block_cols, lanes), jnp.float32),
            pltpu.VMEM((COLS * shard_rows, lanes), jnp.float32),
        ],
        compiler_params=limit(16),
        name="finish",
    )(place, returned, momentum)


def exchange(array):
    return lax.all_to_all(array, COL + REPLICA, split_axis=0, concat_axis=0, tiled=True)


def swap(array):
    return lax.ppermute(array, "core", [(0, 1), (1, 0)])


def local(gradient, second_moment, momentum, left_factor, right_factor, block_of_slot):
    spread = spread_factors(left_factor, right_factor)
    factors = [
        lax.ppermute(shard, ("core",) + REPLICA, factor_pairs(step)) for step, shard in enumerate(spread)
    ]
    moment_new, pieces, place = prepare(block_of_slot, gradient, second_moment, spread[0])
    any_live = jnp.any(block_of_slot >= 0)
    columns = lax.cond(any_live, exchange, jnp.zeros_like, pieces)
    held = together(columns, spread[0], factors)
    parts = precondition(held, swap(held))
    return (finish(place, exchange(parts), momentum), moment_new)


def solution(mesh):
    fine = Mesh(mesh.devices.reshape((2,) * 9), COL + ("core",) + REPLICA)
    fsdp = COL + ("core",)
    in_specs = (
        P(None, fsdp, None, REPLICA),
        P(None, fsdp, None, REPLICA),
        P(None, fsdp, None, REPLICA),
        P(fsdp, REPLICA, None),
        P(fsdp, None, REPLICA),
        P(),
    )
    out_specs = (P(None, fsdp, None, REPLICA), P(None, fsdp, None, REPLICA))
    return jax.shard_map(local, mesh=fine, in_specs=in_specs, out_specs=out_specs, check_vma=False)
```

time: 300 us -> 152 us (0.51)
  waiting for transfers between devices: 105 us -> 5.27 us
  blocking collectives: 145 us -> 97.6 us
  Pallas kernels: 0 us -> 15.3 us
  starting transfers between devices: 10.7 us -> 24.6 us
  between operations: 14.3 us -> 1.38 us
  matrix products: 10.6 us -> 0 us
  local copies, waits for them, and re-layouts: 10.2 us -> 5.12 us
    psum x2 -> x0, blocking collectives: 111 us -> none  [the longest x1 98.6 us: local(): adam_totals = lax.psum(partial_value, ('fsdp', 'replica'))]
    all_gather x2 -> x0, waiting for transfers between devices: 78.1 us -> none  [the longest x1 78 us: local(): lax.all_gather(owner_grad, 'replica', axis=2, tiled=True)]
    all_to_all x1 -> x2, blocking collectives: 34.4 us -> 97.6 us  [exchange(): lax.all_to_all(array, COL + REPLICA, split_axis=0, concat_axis=0, tiled=T...]
    all_to_all x1 -> x0, waiting for transfers between devices: 27.2 us -> none  [local(): lax.all_to_all(grafted, 'fsdp', split_axis=1, concat_axis=0, tiled=True)]
    ppermute x0 -> x5, starting transfers between devices: none -> 24.6 us  [the longest x4 20 us: local(): lax.ppermute(shard, ('core',) + REPLICA, factor_pairs(step))]
    pallas_call x0 -> x5, Pallas kernels: none -> 15.3 us  [the longest x1 6.08 us: precondition(): pl.pallas_call(block_kernel, out_shape=jax.ShapeDtypeStruct((COLS * RING,...]
    all_to_all x1 -> x0, starting transfers between devices: 10.6 us -> none  [local(): lax.all_to_all(grafted, 'fsdp', split_axis=1, concat_axis=0, tiled=True)]
    dot_general x2 -> x0, matrix products: 10.6 us -> none  [the longest x1 5.46 us: local(): jnp.einsum('sij,sjk->sik', left_factor, lax.all_gather(owner_grad, 'repli...]
  transfers between devices with their start and end apart: 3 -> 5, of which waited for: 2 -> 1; matrix products, arithmetic and copies ran while one was open for 1% -> 1% of each run, Pallas kernels for 0% -> 3%
where the time goes in v1:
time: 152 us; the launch traced here: 151 us
  blocking collectives  97.6 us (64%)
  starting transfers between devices  24.6 us (16%)
  Pallas kernels  15.3 us (10%)
  waiting for transfers between devices  5.27 us (3%)
  local copies, waits for them, and re-layouts  5.12 us (3%)
    all_to_all x2, blocking collectives, exchange(): lax.all_to_all(array, COL + REPLICA, split_axis=0, concat_axis=0, tiled=T...  97.6 us
    ppermute x4, starting transfers between devices, local(): lax.ppermute(shard, ('core',) + REPLICA, factor_pairs(step))  20 us
    pallas_call x1, Pallas kernels, precondition(): pl.pallas_call(block_kernel, out_shape=jax.ShapeDtypeStruct((COLS * RING,...  6.08 us
    ppermute x1, waiting for transfers between devices, swap(): return lax.ppermute(array, 'core', [(0, 1), (1, 0)])  5.26 us
    unnamed x11, local copies, waits for them, and re-layouts  5.12 us
    ppermute x1, starting transfers between devices, swap(): return lax.ppermute(array, 'core', [(0, 1), (1, 0)])  4.64 us
    pallas_call x1, Pallas kernels, prepare(): pl.pallas_call(prepare_kernel, out_shape=[jax.ShapeDtypeStruct(second.sha...  4.45 us
  transfers between devices with their start and end apart: 5, of which 1 were waited for; matrix products, arithmetic and copies ran while one was open for 1% of the time, Pallas kernels for 3%

profile of v1, /device:TPU:1, one launch (start us, length us, event | category | flops | bytes accessed | tf_op | source)
XLA Modules:
  0.0 150.6 jit_solution(2624166361662290131)
XLA Ops:
  0.6 0.0 copy-start
  0.6 1.1 copy-done
  1.8 0.0 copy-start.1
  1.8 1.1 copy-done.1
  2.9 1.2 spread_factors.1
  4.1 1.3 collective-permute-start.1
  5.4 12.4 %collective-permute-start.2 = (bf16[16,128,128]{2,1,0:T(8,128)(2,1)}, bf16[16,128,128]{2,1,0:T(8,128)(2,1)S(1)}, u32[]{:S(2)}, u32[]{:S(2)}) collective-permute-start(bf16[16,128,128]{2,1,0:T(8,128)(2,1)} %get-tuple-element.17), channel_id=1, source_target_pairs={{2,0},{6,8},{3,1},{7,9},{4,2},{0,10},{14,12},{10,4},{15,13},{11,5}... | collective-permute-start | bytes 1572872 | tf_op jit(solution)/shard_map/ppermute | solution.py:306
  17.7 1.9 %collective-permute-start.3 = (bf16[16,128,128]{2,1,0:T(8,128)(2,1)S(1)}, bf16[16,128,128]{2,1,0:T(8,128)(2,1)S(1)}, u32[]{:S(2)}, u32[]{:S(2)}) collective-permute-start(bf16[16,128,128]{2,1,0:T(8,128)(2,1)S(1)} %get-tuple-element.18), channel_id=1, source_target_pairs={{3,0},{7,8},{4,1},{0,9},{5,2},{1,10},{15,12},{11,4},{8,13},{12,5},... | collective-permute-start | bytes 1572872 | tf_op jit(solution)/shard_map/ppermute | solution.py:306
  19.7 4.4 %collective-permute-start = (bf16[16,128,128]{2,1,0:T(8,128)(2,1)S(1)}, bf16[16,128,128]{2,1,0:T(8,128)(2,1)S(1)}, u32[]{:S(2)}, u32[]{:S(2)}) collective-permute-start(bf16[16,128,128]{2,1,0:T(8,128)(2,1)S(1)} %get-tuple-element.13.after.own), channel_id=1, source_target_pairs={{4,8},{5,9},{6,10},{8,4},{9,5},{10,6},{20,24},{21,25},{22,26},{24,... | collective-permute-start | bytes 1572872 | tf_op jit(solution)/shard_map/ppermute | solution.py:306
  24.1 0.8 copy.8.slots
  24.9 1.3 compare_reduce_fusion
  26.8 0.0 copy-start.2
  26.8 1.0 copy-done.2
  27.9 0.0 copy-start.3
  27.9 1.0 copy-done.3
  28.9 4.5 %prepare.1 = (bf16[16,16,8,128]{3,2,1,0:T(8,128)(2,1)}, bf16[256,16,128]{2,1,0:T(8,128)(2,1)}, s32[2,128]{1,0:T(2,128)S(1)}) custom-call(s32[64,3]{1,0:T(8,128)S(1)} %copy.8.slots, bf16[16,16,8,128]{3,2,1,0:T(8,128)(2,1)S(1)} %copy-done.2, bf16[16,16,8,128]{3,2,1,0:T(8,128)(2,1)S(1)} %copy-done.3, bf16[16,128,128]{2,1,0:T(8,128)(2,1)S(1)} %get-tuple-element.13.after.own), custom_call_target="tpu_custom_call" | custom-call | tf_op jit(solution)/shard_map/prepare/pallas_call | solution.py:122
  33.4 51.5 %conditional.1 = (bf16[256,16,128]{2,1,0:T(8,128)(2,1)}) conditional(s32[]{:T(128)} %convert_element_type.3, () %tuple.14, bf16[256,16,128]{2,1,0:T(8,128)(2,1)} %get-tuple-element.15), branch_computations={%region_1.0_spmd, %region_2.0_spmd} | conditional | bytes 2097160 | solution.py:310
  33.4 51.5 %all_to_all.9 = bf16[256,16,128]{2,1,0:T(8,128)(2,1)} all-to-all(bf16[256,16,128]{2,1,0:T(8,128)(2,1)} %param.1), channel_id=1, replica_groups=mesh['x1'=2,'x0'=2,'y2'=2,'y1'=2,'y0'=2,'core'=2,'z2'=2,'z1'=2,'z0'=2] {..., dimensions={0} | all-to-all | bytes 2097152 | tf_op jit(solution)/shard_map/cond/branch_1_fun/all_to_all | solution.py:296
  84.9 0.0 collective-permute-done.1.refs_1_
  84.9 0.0 collective-permute-done.2.refs_2_
  84.9 0.0 collective-permute-done.3.refs_3_
  84.9 0.0 collective-permute-done.refs_0_
  84.9 1.4 together.1.own
  86.4 0.0 copy-start.4
  86.4 4.6 %collective-permute-start.4 = (bf16[768,16,128]{2,1,0:T(8,128)(2,1)S(1)}, bf16[768,16,128]{2,1,0:T(8,128)(2,1)S(1)}, u32[]{:S(2)}, u32[]{:S(2)}) collective-permute-start(bf16[768,16,128]{2,1,0:T(8,128)(2,1)S(1)} %together.1.own), channel_id=1, source_target_pairs={{0,8},{8,0},{1,9},{9,1},{2,10},{10,2},{3,11},{11,3},{4,12},{12,4},... | collective-permute-start | bytes 9437192 | tf_op jit(solution)/shard_map/ppermute | solution.py:300
  91.0 5.3 %collective-permute-done.4.swapped = bf16[768,16,128]{2,1,0:T(8,128)(2,1)S(1)} collective-permute-done((bf16[768,16,128]{2,1,0:T(8,128)(2,1)S(1)}, bf16[768,16,128]{2,1,0:T(8,128)(2,1)S(1)}, u32[]{:S(2)}, u32[]{:S(2)}) %collective-permute-start.4) | collective-permute-done | bytes 3145760 | tf_op jit(solution)/shard_map/ppermute | solution.py:300
  96.3 6.1 %precondition.1 = bf16[256,16,128]{2,1,0:T(8,128)(2,1)S(1)} custom-call(bf16[768,16,128]{2,1,0:T(8,128)(2,1)S(1)} %together.1.own, bf16[768,16,128]{2,1,0:T(8,128)(2,1)S(1)} %collective-permute-done.4.swapped), custom_call_target="tpu_custom_call" | custom-call | flops 4294967296 | bytes 10485760 | tf_op jit(solution)/shard_map/precondition/pallas_call | solution.py:240
  102.4 46.1 %all_to_all.10.returned = bf16[256,16,128]{2,1,0:T(8,128)(2,1)S(1)} all-to-all(bf16[256,16,128]{2,1,0:T(8,128)(2,1)S(1)} %precondition.1), channel_id=1, replica_groups=mesh['x1'=2,'x0'=2,'y2'=2,'y1'=2,'y0'=2,'core'=2,'z2'=2,'z1'=2,'z0'=2] {..., dimensions={0} | all-to-all | bytes 2097152 | tf_op jit(solution)/shard_map/all_to_all | solution.py:296
  148.4 0.0 copy-done.4
  148.4 2.2 %finish.1 = bf16[16,16,8,128]{3,2,1,0:T(8,128)(2,1)} custom-call(s32[2,128]{1,0:T(2,128)S(1)} %get-tuple-element.14.place, bf16[256,16,128]{2,1,0:T(8,128)(2,1)S(1)} %all_to_all.10.returned, bf16[16,16,8,128]{3,2,1,0:T(8,128)(2,1)S(1)} %copy-done.4), custom_call_target="tpu_custom_call" | custom-call | tf_op jit(solution)/shard_map/finish/pallas_call | solution.py:281
Async XLA Ops:
  0.6 1.1 copy-start
  1.8 1.1 copy-start.1
  4.1 80.8 %collective-permute-start.1 = (bf16[16,128,128]{2,1,0:T(8,128)(2,1)}, bf16[16,128,128]{2,1,0:T(8,128)(2,1)S(1)}, u32[]{:S(2)}, u32[]{:S(2)}) collective-permute-start(bf16[16,128,128]{2,1,0:T(8,128)(2,1)} %get-tuple-element.16), channel_id=1, source_target_pairs={{1,0},{5,8},{2,1},{6,9},{3,2},{7,10},{13,12},{9,4},{14,13},{10,5},... | collective-permute-start | bytes 1572872 | tf_op jit(solution)/shard_map/ppermute | solution.py:306
  5.4 79.5 %collective-permute-start.2 = (bf16[16,128,128]{2,1,0:T(8,128)(2,1)}, bf16[16,128,128]{2,1,0:T(8,128)(2,1)S(1)}, u32[]{:S(2)}, u32[]{:S(2)}) collective-permute-start(bf16[16,128,128]{2,1,0:T(8,128)(2,1)} %get-tuple-element.17), channel_id=1, source_target_pairs={{2,0},{6,8},{3,1},{7,9},{4,2},{0,10},{14,12},{10,4},{15,13},{11,5}... | collective-permute-start | bytes 1572872 | tf_op jit(solution)/shard_map/ppermute | solution.py:306
  17.7 67.2 %collective-permute-start.3 = (bf16[16,128,128]{2,1,0:T(8,128)(2,1)S(1)}, bf16[16,128,128]{2,1,0:T(8,128)(2,1)S(1)}, u32[]{:S(2)}, u32[]{:S(2)}) collective-permute-start(bf16[16,128,128]{2,1,0:T(8,128)(2,1)S(1)} %get-tuple-element.18), channel_id=1, source_target_pairs={{3,0},{7,8},{4,1},{0,9},{5,2},{1,10},{15,12},{11,4},{8,13},{12,5},... | collective-permute-start | bytes 1572872 | tf_op jit(solution)/shard_map/ppermute | solution.py:306
  19.7 65.2 %collective-permute-start = (bf16[16,128,128]{2,1,0:T(8,128)(2,1)S(1)}, bf16[16,128,128]{2,1,0:T(8,128)(2,1)S(1)}, u32[]{:S(2)}, u32[]{:S(2)}) collective-permute-start(bf16[16,128,128]{2,1,0:T(8,128)(2,1)S(1)} %get-tuple-element.13.after.own), channel_id=1, source_target_pairs={{4,8},{5,9},{6,10},{8,4},{9,5},{10,6},{20,24},{21,25},{22,26},{24,... | collective-permute-start | bytes 1572872 | tf_op jit(solution)/shard_map/ppermute | solution.py:306
  26.8 1.0 copy-start.2
  27.9 1.0 copy-start.3
  86.4 62.1 %copy-start.4 = (bf16[16,16,8,128]{3,2,1,0:T(8,128)(2,1)S(1)}, bf16[16,16,8,128]{3,2,1,0:T(8,128)(2,1)}, u32[]{:S(2)}) copy-start(bf16[16,16,8,128]{3,2,1,0:T(8,128)(2,1)} %momentum.1) | copy-start | bytes 1572868
  86.4 9.9 %collective-permute-start.4 = (bf16[768,16,128]{2,1,0:T(8,128)(2,1)S(1)}, bf16[768,16,128]{2,1,0:T(8,128)(2,1)S(1)}, u32[]{:S(2)}, u32[]{:S(2)}) collective-permute-start(bf16[768,16,128]{2,1,0:T(8,128)(2,1)S(1)} %together.1.own), channel_id=1, source_target_pairs={{0,8},{8,0},{1,9},{9,1},{2,10},{10,2},{3,11},{11,3},{4,12},{12,4},... | collective-permute-start | bytes 9437192 | tf_op jit(solution)/shard_map/ppermute | solution.py:300

commit v2 on v1

--- a/solution.py
+++ b/solution.py
@@ -11,16 +11,18 @@
 ADAM_EPS = 1e-08
 NORM_EPS = 1e-06
 
-COL = ("x1", "x0", "y2", "y1", "y0")
-REPLICA = ("z2", "z1", "z0")
+COL = ("x", "y")
+SHAPE = (4, 8, 2, 8)
 RING = 8
 COLS = 32
 SLOTS = 3
 PLACES = 4
 CORES = 2
 NOTE = 3
+CHUNKS = 4
 
 ANY = pl.BlockSpec(memory_space=pl.ANY)
+HBM = pl.BlockSpec(memory_space=pltpu.HBM)
 VMEM = pl.BlockSpec(memory_space=pltpu.VMEM)
 SMEM = pl.BlockSpec(memory_space=pltpu.SMEM)
 
@@ -50,17 +52,26 @@
     return pairs
 
 
-def factor_kernel(left, right, *outs):
+def factor_kernel(left, right, *refs):
+    outs, held_left, held_right, sems = refs[:PLACES], *refs[PLACES:]
     part = left.shape[1]
-    here = lax.axis_index(REPLICA)
+    here = lax.axis_index("replica")
+    copies = []
+    for s in range(SLOTS):
+        copies.append(pltpu.make_async_copy(left.at[s], held_left.at[s], sems.at[0, s]))
+        copies.append(pltpu.make_async_copy(right.at[s], held_right.at[s], sems.at[1, s]))
+    for copy in copies:
+        copy.start()
+    for copy in copies:
+        copy.wait()
     for step in range(PLACES):
         slot = lax.rem(here - step + RING, PLACES)
 
         @pl.when(slot < SLOTS)
         def _():
             for j in range(RING):
-                outs[step][j] = left[slot, :, j * part : (j + 1) * part]
-                outs[step][RING + j] = right[slot, j * part : (j + 1) * part, :]
+                outs[step][j] = held_left[slot, :, j * part : (j + 1) * part]
+                outs[step][RING + j] = held_right[slot, j * part : (j + 1) * part, :]
 
 
 def spread_factors(left, right):
@@ -68,33 +79,52 @@
     return pl.pallas_call(
         factor_kernel,
         out_shape=[jax.ShapeDtypeStruct((2 * RING, part, part), left.dtype)] * PLACES,
-        in_specs=[VMEM, VMEM],
+        in_specs=[HBM, HBM],
         out_specs=[VMEM] * PLACES,
-        compiler_params=limit(16),
+        scratch_shapes=[
+            pltpu.VMEM(left.shape, left.dtype),
+            pltpu.VMEM(right.shape, right.dtype),
+            pltpu.SemaphoreType.DMA((2, SLOTS)),
+        ],
+        compiler_params=limit(63),
         name="spread_factors",
     )(left, right)
 
 
-def prepare_kernel(slots, gradient, second, after, moment, pieces, place, wide, square, notes):
+def prepare_kernel(slots, gradient, second, after, moment, pieces, place, *scratch):
+    held_gradient, held_second, held_moment, wide, square, notes, sems = scratch
     block_rows, shard_rows, block_cols, lanes = gradient.shape
     per_row = shard_rows * block_cols
+    chunk = block_rows // CHUNKS
+    chunks = [pl.ds(at * chunk, chunk) for at in range(CHUNKS)]
+    first, second_in, out = [], [], []
+    for at, rows in enumerate(chunks):
+        first.append(pltpu.make_async_copy(gradient.at[rows], held_gradient.at[rows], sems.at[0, at]))
+        second_in.append(pltpu.make_async_copy(second.at[rows], held_second.at[rows], sems.at[1, at]))
+        out.append(pltpu.make_async_copy(held_moment.at[rows], moment.at[rows], sems.at[2, at]))
+        first[at].start()
+        second_in[at].start()
 
     def adam(i, carry):
-        g = gradient[i].astype(jnp.float32)
-        v = BETA_TWO * second[i].astype(jnp.float32) + (1.0 - BETA_TWO) * g * g
-        moment[i] = v.astype(moment.dtype)
+        g = held_gradient[i].astype(jnp.float32)
+        v = BETA_TWO * held_second[i].astype(jnp.float32) + (1.0 - BETA_TWO) * g * g
+        held_moment[i] = v.astype(moment.dtype)
         step = g / (jnp.sqrt(v) + ADAM_EPS)
         square[pl.ds(pl.multiple_of(i * block_cols, block_cols), block_cols), :] = jnp.sum(step * step, axis=0)
         wide[pl.ds(pl.multiple_of(i * per_row, per_row), per_row), :] = g.reshape(per_row, lanes)
         return carry
 
-    lax.fori_loop(0, block_rows, adam, 0)
+    for at in range(CHUNKS):
+        first[at].wait()
+        second_in[at].wait()
+        lax.fori_loop(at * chunk, (at + 1) * chunk, adam, 0)
+        out[at].start()
     notes[...] = jnp.zeros(notes.shape, notes.dtype)
 
     def column(col, carry):
         for c in range(CORES):
             for s in range(SLOTS):
-                held = slots[col * CORES + c, s]
+                held = slots[s, col * CORES + c]
                 block = jnp.maximum(held, 0)
                 i = lax.div(block, block_cols)
                 j = lax.rem(block, block_cols)
@@ -114,6 +144,8 @@
         return carry
 
     lax.fori_loop(0, COLS, column, 0)
+    for copy in out:
+        copy.wait()
 
 
 def prepare(slots, gradient, second, after):
@@ -126,14 +158,18 @@
             jax.ShapeDtypeStruct((COLS * RING, shard_rows, lanes), gradient.dtype),
             jax.ShapeDtypeStruct((2, block_count), jnp.int32),
         ],
-        in_specs=[SMEM, VMEM, VMEM, ANY],
-        out_specs=[VMEM, VMEM, SMEM],
+        in_specs=[SMEM, HBM, HBM, ANY],
+        out_specs=[HBM, VMEM, SMEM],
         scratch_shapes=[
+            pltpu.VMEM(gradient.shape, gradient.dtype),
+            pltpu.VMEM(second.shape, second.dtype),
+            pltpu.VMEM(second.shape, second.dtype),
             pltpu.VMEM((block_count * shard_rows, lanes), jnp.float32),
             pltpu.VMEM((block_count, lanes), jnp.float32),
             pltpu.VMEM((shard_rows, lanes), jnp.float32),
-        ],
-        compiler_params=limit(16),
+            pltpu.SemaphoreType.DMA((3, CHUNKS)),
+        ],
+        compiler_params=limit(63),
         name="prepare",
     )(slots, gradient, second, after)
 
@@ -142,7 +178,7 @@
     factors, out = refs[:PLACES], refs[PLACES]
     count = columns.shape[0]
     size = own.shape[0] * own.shape[1] // columns.shape[1]
-    at_home = lax.div(lax.axis_index(REPLICA), PLACES) == lax.axis_index("core")
+    at_home = lax.div(lax.axis_index("replica"), PLACES) == lax.axis_index("core")
     out[:count] = columns[...]
     for step in range(1, PLACES):
         out[count + step * size : count + (step + 1) * size] = factors[step][...].reshape((size,) + columns.shape[1:])
@@ -175,7 +211,7 @@
     count = COLS * RING
     groups = part // rows
     core = lax.axis_index("core")
-    here = lax.axis_index(REPLICA)
+    here = lax.axis_index("replica")
     place = lax.rem(here, PLACES)
 
     @pl.when(place < SLOTS)
@@ -293,7 +329,7 @@
 
 
 def exchange(array):
-    return lax.all_to_all(array, COL + REPLICA, split_axis=0, concat_axis=0, tiled=True)
+    return lax.all_to_all(array, COL + ("replica",), split_axis=0, concat_axis=0, tiled=True)
 
 
 def swap(array):
@@ -303,26 +339,25 @@
 def local(gradient, second_moment, momentum, left_factor, right_factor, block_of_slot):
     spread = spread_factors(left_factor, right_factor)
     factors = [
-        lax.ppermute(shard, ("core",) + REPLICA, factor_pairs(step)) for step, shard in enumerate(spread)
+        lax.ppermute(shard, ("core", "replica"), factor_pairs(step)) for step, shard in enumerate(spread)
     ]
-    moment_new, pieces, place = prepare(block_of_slot, gradient, second_moment, spread[0])
-    any_live = jnp.any(block_of_slot >= 0)
-    columns = lax.cond(any_live, exchange, jnp.zeros_like, pieces)
+    moment_new, pieces, place = prepare(block_of_slot.T, gradient, second_moment, spread[0])
+    columns = lax.cond(block_of_slot[0, 0] >= -1, exchange, jnp.zeros_like, pieces)
     held = together(columns, spread[0], factors)
     parts = precondition(held, swap(held))
     return (finish(place, exchange(parts), momentum), moment_new)
 
 
 def solution(mesh):
-    fine = Mesh(mesh.devices.reshape((2,) * 9), COL + ("core",) + REPLICA)
+    fine = Mesh(mesh.devices.reshape(SHAPE), COL + ("core", "replica"))
     fsdp = COL + ("core",)
     in_specs = (
-        P(None, fsdp, None, REPLICA),
-        P(None, fsdp, None, REPLICA),
-        P(None, fsdp, None, REPLICA),
-        P(fsdp, REPLICA, None),
-        P(fsdp, None, REPLICA),
+        P(None, fsdp, None, "replica"),
+        P(None, fsdp, None, "replica"),
+        P(None, fsdp, None, "replica"),
+        P(fsdp, "replica", None),
+        P(fsdp, None, "replica"),
         P(),
     )
-    out_specs = (P(None, fsdp, None, REPLICA), P(None, fsdp, None, REPLICA))
+    out_specs = (P(None, fsdp, None, "replica"), P(None, fsdp, None, "replica"))
     return jax.shard_map(local, mesh=fine, in_specs=in_specs, out_specs=out_specs, check_vma=False)

time: 152 us -> 152 us (level)
  local copies, waits for them, and re-layouts: 5.12 us -> 1.21 us
  Pallas kernels: 15.3 us -> 18.1 us
    unnamed x11 -> x6, local copies, waits for them, and re-layouts: 5.12 us -> 0.02 us
    pallas_call x1, Pallas kernels: 1.17 us -> 2.91 us  [spread_factors(): pl.pallas_call(factor_kernel, out_shape=[jax.ShapeDtypeStruct((2 * RING,...]
  transfers between devices with their start and end apart: 5 -> 5, of which waited for: 1 -> 2; matrix products, arithmetic and copies ran while one was open for 1% -> 1% of each run, Pallas kernels for 3% -> 3%
where the time goes in v2:
time: 152 us; the launch traced here: 151 us
  blocking collectives  98.6 us (65%)
  starting transfers between devices  25.4 us (17%)
  Pallas kernels  18.1 us (12%)
  waiting for transfers between devices  5.86 us (4%)
    all_to_all x2, blocking collectives, exchange(): lax.all_to_all(array, COL + ('replica',), split_axis=0, concat_axis=0, ti...  98.6 us
    ppermute x4, starting transfers between devices, local(): lax.ppermute(shard, ('core', 'replica'), factor_pairs(step))  20.1 us
    pallas_call x1, Pallas kernels, precondition(): pl.pallas_call(block_kernel, out_shape=jax.ShapeDtypeStruct((COLS * RING,...  6.14 us
    ppermute x1, starting transfers between devices, swap(): return lax.ppermute(array, 'core', [(0, 1), (1, 0)])  5.27 us
    ppermute x1, waiting for transfers between devices, swap(): return lax.ppermute(array, 'core', [(0, 1), (1, 0)])  5.26 us
    pallas_call x1, Pallas kernels, prepare(): pl.pallas_call(prepare_kernel, out_shape=[jax.ShapeDtypeStruct(second.sha...  5.08 us
  transfers between devices with their start and end apart: 5, of which 2 were waited for; matrix products, arithmetic and copies ran while one was open for 1% of the time, Pallas kernels for 3%

profile of v2, /device:TPU:1, one launch (start us, length us, event | category | flops | bytes accessed | tf_op | source)
XLA Modules:
  0.0 150.5 jit_solution(7031002077165432068)
XLA Ops:
  0.6 2.9 %spread_factors.1 = (bf16[16,128,128]{2,1,0:T(8,128)(2,1)}, bf16[16,128,128]{2,1,0:T(8,128)(2,1)}, bf16[16,128,128]{2,1,0:T(8,128)(2,1)}, bf16[16,128,128]{2,1,0:T(8,128)(2,1)}) custom-call(bf16[3,128,1024]{2,1,0:T(8,128)(2,1)} %left.1, bf16[3,1024,128]{2,1,0:T(8,128)(2,1)} %right.1), custom_call_target="tpu_custom_call" | custom-call | tf_op jit(solution)/shard_map/spread_factors/pallas_call | solution.py:79
  3.6 0.0 copy-start
  3.6 1.4 collective-permute-start.1
  5.0 12.4 %collective-permute-start.2 = (bf16[16,128,128]{2,1,0:T(8,128)(2,1)}, bf16[16,128,128]{2,1,0:T(8,128)(2,1)}, u32[]{:S(2)}, u32[]{:S(2)}) collective-permute-start(bf16[16,128,128]{2,1,0:T(8,128)(2,1)} %get-tuple-element.17), channel_id=1, source_target_pairs={{2,0},{6,8},{3,1},{7,9},{4,2},{0,10},{14,12},{10,4},{15,13},{11,5}... | collective-permute-start | bytes 1572872 | tf_op jit(solution)/shard_map/ppermute | solution.py:342
  17.4 1.9 %collective-permute-start.3 = (bf16[16,128,128]{2,1,0:T(8,128)(2,1)}, bf16[16,128,128]{2,1,0:T(8,128)(2,1)}, u32[]{:S(2)}, u32[]{:S(2)}) collective-permute-start(bf16[16,128,128]{2,1,0:T(8,128)(2,1)} %get-tuple-element.18), channel_id=1, source_target_pairs={{3,0},{7,8},{4,1},{0,9},{5,2},{1,10},{15,12},{11,4},{8,13},{12,5},... | collective-permute-start | bytes 1572872 | tf_op jit(solution)/shard_map/ppermute | solution.py:342
  19.3 4.4 %collective-permute-start = (bf16[16,128,128]{2,1,0:T(8,128)(2,1)}, bf16[16,128,128]{2,1,0:T(8,128)(2,1)}, u32[]{:S(2)}, u32[]{:S(2)}) collective-permute-start(bf16[16,128,128]{2,1,0:T(8,128)(2,1)} %get-tuple-element.13.after.own), channel_id=1, source_target_pairs={{4,8},{5,9},{6,10},{8,4},{9,5},{10,6},{20,24},{21,25},{22,26},{24,... | collective-permute-start | bytes 1572872 | tf_op jit(solution)/shard_map/ppermute | solution.py:342
  23.7 1.2 slice.3
  25.6 5.1 %prepare.1 = (bf16[16,16,8,128]{3,2,1,0:T(8,128)(2,1)}, bf16[256,16,128]{2,1,0:T(8,128)(2,1)}, s32[2,128]{1,0:T(2,128)}) custom-call(s32[3,64]{1,0:T(4,128)} %bitcast.2, bf16[16,16,8,128]{3,2,1,0:T(8,128)(2,1)} %gradient.1, bf16[16,16,8,128]{3,2,1,0:T(8,128)(2,1)} %second.1, bf16[16,128,128]{2,1,0:T(8,128)(2,1)} %get-tuple-element.13.after.own), custom_call_target="tpu_custom_call" | custom-call | tf_op jit(solution)/shard_map/prepare/pallas_call | solution.py:154
  30.7 52.5 %conditional.1 = (bf16[256,16,128]{2,1,0:T(8,128)(2,1)S(1)}) conditional(s32[]{:T(128)} %bitcast.1, () %tuple.14, bf16[256,16,128]{2,1,0:T(8,128)(2,1)} %get-tuple-element.15), branch_computations={%region_0.0_spmd, %region_1.0_spmd} | conditional | bytes 2097160 | solution.py:345
  30.7 52.5 %all_to_all.9 = bf16[256,16,128]{2,1,0:T(8,128)(2,1)S(1)} all-to-all(bf16[256,16,128]{2,1,0:T(8,128)(2,1)} %param.1), channel_id=1, replica_groups=mesh['x'=4,'y'=8,'core'=2,'replica'=8] {'x','y','replica'}, dimensions={0} | all-to-all | bytes 2097152 | tf_op jit(solution)/shard_map/cond/branch_1_fun/all_to_all | solution.py:332
  83.2 0.0 collective-permute-done.1.refs_1_
  83.2 0.0 collective-permute-done.2.refs_2_
  83.2 0.6 collective-permute-done.3.refs_3_
  83.8 0.0 collective-permute-done.refs_0_
  83.8 0.0 copy-done
  83.8 1.7 %together.1.own = bf16[768,16,128]{2,1,0:T(8,128)(2,1)S(1)} custom-call(bf16[256,16,128]{2,1,0:T(8,128)(2,1)S(1)} %get-tuple-element.20.columns, bf16[16,128,128]{2,1,0:T(8,128)(2,1)S(1)} %copy-done, bf16[16,128,128]{2,1,0:T(8,128)(2,1)} %collective-permute-done.refs_0_, bf16[16,128,128]{2,1,0:T(8,128)(2,1)} %collective-permute-done.1.refs_1_, ...), custom_call_target="tpu_custom_call" | custom-call | tf_op jit(solution)/shard_map/together/pallas_call | solution.py:198
  85.5 0.0 copy-start.1
  85.5 0.0 copy-start.2
  85.5 5.3 %collective-permute-start.4 = (bf16[768,16,128]{2,1,0:T(8,128)(2,1)S(1)}, bf16[768,16,128]{2,1,0:T(8,128)(2,1)S(1)}, u32[]{:S(2)}, u32[]{:S(2)}) collective-permute-start(bf16[768,16,128]{2,1,0:T(8,128)(2,1)S(1)} %together.1.own), channel_id=1, source_target_pairs={{0,8},{8,0},{1,9},{9,1},{2,10},{10,2},{3,11},{11,3},{4,12},{12,4},... | collective-permute-start | bytes 9437192 | tf_op jit(solution)/shard_map/ppermute | solution.py:336
  90.8 5.3 %collective-permute-done.4.swapped = bf16[768,16,128]{2,1,0:T(8,128)(2,1)S(1)} collective-permute-done((bf16[768,16,128]{2,1,0:T(8,128)(2,1)S(1)}, bf16[768,16,128]{2,1,0:T(8,128)(2,1)S(1)}, u32[]{:S(2)}, u32[]{:S(2)}) %collective-permute-start.4) | collective-permute-done | bytes 3145760 | tf_op jit(solution)/shard_map/ppermute | solution.py:336
  96.1 6.1 %precondition.1 = bf16[256,16,128]{2,1,0:T(8,128)(2,1)S(1)} custom-call(bf16[768,16,128]{2,1,0:T(8,128)(2,1)S(1)} %together.1.own, bf16[768,16,128]{2,1,0:T(8,128)(2,1)S(1)} %collective-permute-done.4.swapped), custom_call_target="tpu_custom_call" | custom-call | flops 4294967296 | bytes 10485760 | tf_op jit(solution)/shard_map/precondition/pallas_call | solution.py:276
  102.2 46.1 %all_to_all.10.returned = bf16[256,16,128]{2,1,0:T(8,128)(2,1)S(1)} all-to-all(bf16[256,16,128]{2,1,0:T(8,128)(2,1)S(1)} %precondition.1), channel_id=1, replica_groups=mesh['x'=4,'y'=8,'core'=2,'replica'=8] {'x','y','replica'}, dimensions={0} | all-to-all | bytes 2097152 | tf_op jit(solution)/shard_map/all_to_all | solution.py:332
  148.3 0.0 copy-done.1
  148.3 0.0 copy-done.2
  148.3 2.2 %finish.1 = bf16[16,16,8,128]{3,2,1,0:T(8,128)(2,1)} custom-call(s32[2,128]{1,0:T(2,128)S(1)} %copy-done.2, bf16[256,16,128]{2,1,0:T(8,128)(2,1)S(1)} %all_to_all.10.returned, bf16[16,16,8,128]{3,2,1,0:T(8,128)(2,1)S(1)} %copy-done.1), custom_call_target="tpu_custom_call" | custom-call | tf_op jit(solution)/shard_map/finish/pallas_call | solution.py:317
Async XLA Ops:
  3.6 80.2 %copy-start = (bf16[16,128,128]{2,1,0:T(8,128)(2,1)S(1)}, bf16[16,128,128]{2,1,0:T(8,128)(2,1)}, u32[]{:S(2)}) copy-start(bf16[16,128,128]{2,1,0:T(8,128)(2,1)} %get-tuple-element.13.after.own) | copy-start | bytes 1572868
  3.6 79.6 %collective-permute-start.1 = (bf16[16,128,128]{2,1,0:T(8,128)(2,1)}, bf16[16,128,128]{2,1,0:T(8,128)(2,1)}, u32[]{:S(2)}, u32[]{:S(2)}) collective-permute-start(bf16[16,128,128]{2,1,0:T(8,128)(2,1)} %get-tuple-element.16), channel_id=1, source_target_pairs={{1,0},{5,8},{2,1},{6,9},{3,2},{7,10},{13,12},{9,4},{14,13},{10,5},... | collective-permute-start | bytes 1572872 | tf_op jit(solution)/shard_map/ppermute | solution.py:342
  5.0 78.2 %collective-permute-start.2 = (bf16[16,128,128]{2,1,0:T(8,128)(2,1)}, bf16[16,128,128]{2,1,0:T(8,128)(2,1)}, u32[]{:S(2)}, u32[]{:S(2)}) collective-permute-start(bf16[16,128,128]{2,1,0:T(8,128)(2,1)} %get-tuple-element.17), channel_id=1, source_target_pairs={{2,0},{6,8},{3,1},{7,9},{4,2},{0,10},{14,12},{10,4},{15,13},{11,5}... | collective-permute-start | bytes 1572872 | tf_op jit(solution)/shard_map/ppermute | solution.py:342
  17.4 66.4 %collective-permute-start.3 = (bf16[16,128,128]{2,1,0:T(8,128)(2,1)}, bf16[16,128,128]{2,1,0:T(8,128)(2,1)}, u32[]{:S(2)}, u32[]{:S(2)}) collective-permute-start(bf16[16,128,128]{2,1,0:T(8,128)(2,1)} %get-tuple-element.18), channel_id=1, source_target_pairs={{3,0},{7,8},{4,1},{0,9},{5,2},{1,10},{15,12},{11,4},{8,13},{12,5},... | collective-permute-start | bytes 1572872 | tf_op jit(solution)/shard_map/ppermute | solution.py:342
  19.3 64.5 %collective-permute-start = (bf16[16,128,128]{2,1,0:T(8,128)(2,1)}, bf16[16,128,128]{2,1,0:T(8,128)(2,1)}, u32[]{:S(2)}, u32[]{:S(2)}) collective-permute-start(bf16[16,128,128]{2,1,0:T(8,128)(2,1)} %get-tuple-element.13.after.own), channel_id=1, source_target_pairs={{4,8},{5,9},{6,10},{8,4},{9,5},{10,6},{20,24},{21,25},{22,26},{24,... | collective-permute-start | bytes 1572872 | tf_op jit(solution)/shard_map/ppermute | solution.py:342
  85.5 62.8 %copy-start.1 = (bf16[16,16,8,128]{3,2,1,0:T(8,128)(2,1)S(1)}, bf16[16,16,8,128]{3,2,1,0:T(8,128)(2,1)}, u32[]{:S(2)}) copy-start(bf16[16,16,8,128]{3,2,1,0:T(8,128)(2,1)} %momentum.1) | copy-start | bytes 1572868
  85.5 62.8 %copy-start.2 = (s32[2,128]{1,0:T(2,128)S(1)}, s32[2,128]{1,0:T(2,128)}, u32[]{:S(2)}) copy-start(s32[2,128]{1,0:T(2,128)} %get-tuple-element.14.place) | copy-start | bytes 3076
  85.5 10.5 %collective-permute-start.4 = (bf16[768,16,128]{2,1,0:T(8,128)(2,1)S(1)}, bf16[768,16,128]{2,1,0:T(8,128)(2,1)S(1)}, u32[]{:S(2)}, u32[]{:S(2)}) collective-permute-start(bf16[768,16,128]{2,1,0:T(8,128)(2,1)S(1)} %together.1.own), channel_id=1, source_target_pairs={{0,8},{8,0},{1,9},{9,1},{2,10},{10,2},{3,11},{11,3},{4,12},{12,4},... | collective-permute-start | bytes 9437192 | tf_op jit(solution)/shard_map/ppermute | solution.py:336

commit v3 on v2

--- a/solution.py
+++ b/solution.py
@@ -11,8 +11,6 @@
 ADAM_EPS = 1e-08
 NORM_EPS = 1e-06
 
-COL = ("x", "y")
-SHAPE = (4, 8, 2, 8)
 RING = 8
 COLS = 32
 SLOTS = 3
@@ -20,6 +18,7 @@
 CORES = 2
 NOTE = 3
 CHUNKS = 4
+DIRECT = 2
 
 ANY = pl.BlockSpec(memory_space=pl.ANY)
 HBM = pl.BlockSpec(memory_space=pltpu.HBM)
@@ -48,7 +47,21 @@
             near, far = (root + step) % RING, (root + step + PLACES) % RING
             if step > 0:
                 pairs.append((c * RING + near, c * RING + root))
-            pairs.append((c * RING + far, (1 - c) * RING + root))
+                pairs.append((c * RING + far, (1 - c) * RING + root))
+            elif s == DIRECT:
+                pairs.append((c * RING + far, (1 - c) * RING + root))
+            else:
+                pairs.append((c * RING + far, c * RING + root + 1))
+    return pairs
+
+
+def relay_pairs():
+    pairs = []
+    for c in range(CORES):
+        for s in range(SLOTS):
+            root = PLACES * c + s
+            if s != DIRECT:
+                pairs.append((c * RING + root + 1, (1 - c) * RING + root))
     return pairs
 
 
@@ -174,35 +187,56 @@
     )(slots, gradient, second, after)
 
 
-def together_kernel(columns, own, *refs):
+def released_kernel(*refs):
+    pass
+
+
+def released(array, other):
+    return pl.pallas_call(
+        released_kernel,
+        out_shape=jax.ShapeDtypeStruct(array.shape, array.dtype),
+        in_specs=[ANY, ANY],
+        out_specs=ANY,
+        input_output_aliases={0: 0},
+        name="released",
+    )(array, other)
+
+
+def together_kernel(columns, own, relayed, *refs):
     factors, out = refs[:PLACES], refs[PLACES]
-    count = columns.shape[0]
-    size = own.shape[0] * own.shape[1] // columns.shape[1]
-    at_home = lax.div(lax.axis_index("replica"), PLACES) == lax.axis_index("core")
+    count, rows, part = columns.shape
+    size = own.shape[0] * own.shape[1] // rows
+    here = lax.axis_index("replica")
+    at_home = lax.div(here, PLACES) == lax.axis_index("core")
+    direct = lax.rem(here, PLACES) == DIRECT
     out[:count] = columns[...]
     for step in range(1, PLACES):
-        out[count + step * size : count + (step + 1) * size] = factors[step][...].reshape((size,) + columns.shape[1:])
+        out[count + step * size : count + (step + 1) * size] = factors[step][...].reshape(size, rows, part)
 
     @pl.when(at_home)
     def _():
-        out[count : count + size] = own[...].reshape((size,) + columns.shape[1:])
-
-    @pl.when(jnp.logical_not(at_home))
-    def _():
-        out[count : count + size] = factors[0][...].reshape((size,) + columns.shape[1:])
-
-
-def together(columns, own, factors):
+        out[count : count + size] = own[...].reshape(size, rows, part)
+
+    @pl.when(jnp.logical_not(at_home) & direct)
+    def _():
+        out[count : count + size] = factors[0][...].reshape(size, rows, part)
+
+    @pl.when(jnp.logical_not(at_home) & jnp.logical_not(direct))
+    def _():
+        out[count : count + size] = relayed[...].reshape(size, rows, part)
+
+
+def together(columns, shards):
     count, rows, part = columns.shape
-    count += PLACES * own.shape[0] * own.shape[1] // rows
+    count += PLACES * shards[0].shape[0] * shards[0].shape[1] // rows
     return pl.pallas_call(
         together_kernel,
         out_shape=jax.ShapeDtypeStruct((count, rows, part), columns.dtype),
-        in_specs=[VMEM] * (2 + PLACES),
+        in_specs=[VMEM] * (1 + len(shards)),
         out_specs=VMEM,
         compiler_params=limit(16),
         name="together",
-    )(columns, own, *factors)
+    )(columns, *shards)
 
 
 def block_kernel(own, swapped, out, lf, rf, grad, half, full, notes):
@@ -329,7 +363,7 @@
 
 
 def exchange(array):
-    return lax.all_to_all(array, COL + ("replica",), split_axis=0, concat_axis=0, tiled=True)
+    return lax.all_to_all(array, ("col", "replica"), split_axis=0, concat_axis=0, tiled=True)
 
 
 def swap(array):
@@ -338,19 +372,21 @@
 
 def local(gradient, second_moment, momentum, left_factor, right_factor, block_of_slot):
     spread = spread_factors(left_factor, right_factor)
-    factors = [
-        lax.ppermute(shard, ("core", "replica"), factor_pairs(step)) for step, shard in enumerate(spread)
-    ]
+    line = ("core", "replica")
+    factors = [lax.ppermute(shard, line, factor_pairs(step)) for step, shard in enumerate(spread)]
+
     moment_new, pieces, place = prepare(block_of_slot.T, gradient, second_moment, spread[0])
-    columns = lax.cond(block_of_slot[0, 0] >= -1, exchange, jnp.zeros_like, pieces)
-    held = together(columns, spread[0], factors)
+    factors[0] = released(factors[0], pieces)
+    relayed = lax.ppermute(factors[0], line, relay_pairs())
+    columns = lax.cond(lax.axis_index("core") < CORES, exchange, jnp.zeros_like, pieces)
+    held = together(columns, [spread[0], relayed] + factors)
     parts = precondition(held, swap(held))
     return (finish(place, exchange(parts), momentum), moment_new)
 
 
 def solution(mesh):
-    fine = Mesh(mesh.devices.reshape(SHAPE), COL + ("core", "replica"))
-    fsdp = COL + ("core",)
+    fine = Mesh(mesh.devices.reshape(COLS, CORES, RING), ("col", "core", "replica"))
+    fsdp = ("col", "core")
     in_specs = (
         P(None, fsdp, None, "replica"),
         P(None, fsdp, None, "replica"),

time: 152 us -> 152 us (level)
  blocking collectives: 98.6 us -> 102 us
    all_to_all x2, blocking collectives: 98.6 us -> 102 us  [exchange(): lax.all_to_all(array, ('col', 'replica'), split_axis=0, concat_axis=0, ti...]
    ppermute x4 -> x5, starting transfers between devices: 20.1 us -> 18.7 us  [the longest x4 17.4 us: local(): lax.ppermute(shard, line, factor_pairs(step))]
  transfers between devices with their start and end apart: 5 -> 6, of which waited for: 2 -> 1; matrix products, arithmetic and copies ran while one was open for 1% -> 0% of each run, Pallas kernels for 3% -> 3%
where the time goes in v3:
time: 152 us; the launch traced here: 150 us
  blocking collectives  102 us (67%)
  starting transfers between devices  23.9 us (16%)
  Pallas kernels  18.2 us (12%)
  waiting for transfers between devices  5.28 us (3%)
    all_to_all x2, blocking collectives, exchange(): lax.all_to_all(array, ('col', 'replica'), split_axis=0, concat_axis=0, ti...  102 us
    ppermute x4, starting transfers between devices, local(): lax.ppermute(shard, line, factor_pairs(step))  17.4 us
    pallas_call x1, Pallas kernels, precondition(): pl.pallas_call(block_kernel, out_shape=jax.ShapeDtypeStruct((COLS * RING,...  6.14 us
    ppermute x1, waiting for transfers between devices, swap(): return lax.ppermute(array, 'core', [(0, 1), (1, 0)])  5.26 us
    pallas_call x1, Pallas kernels, prepare(): pl.pallas_call(prepare_kernel, out_shape=[jax.ShapeDtypeStruct(second.sha...  5.2 us
    ppermute x1, starting transfers between devices, swap(): return lax.ppermute(array, 'core', [(0, 1), (1, 0)])  5.16 us
  transfers between devices with their start and end apart: 6, of which 1 were waited for; matrix products, arithmetic and copies ran while one was open for 0% of the time, Pallas kernels for 3%

profile of v3, /device:TPU:1, one launch (start us, length us, event | category | flops | bytes accessed | tf_op | source)
XLA Modules:
  0.0 150.0 jit_solution(15832498351838762440)
XLA Ops:
  0.6 2.9 %spread_factors.1 = (bf16[16,128,128]{2,1,0:T(8,128)(2,1)}, bf16[16,128,128]{2,1,0:T(8,128)(2,1)}, bf16[16,128,128]{2,1,0:T(8,128)(2,1)}, bf16[16,128,128]{2,1,0:T(8,128)(2,1)}) custom-call(bf16[3,128,1024]{2,1,0:T(8,128)(2,1)} %left.1, bf16[3,1024,128]{2,1,0:T(8,128)(2,1)} %right.1), custom_call_target="tpu_custom_call" | custom-call | tf_op jit(solution)/shard_map/spread_factors/pallas_call | solution.py:92
  3.5 12.3 %collective-permute-start = (bf16[16,128,128]{2,1,0:T(8,128)(2,1)}, bf16[16,128,128]{2,1,0:T(8,128)(2,1)}, u32[]{:S(2)}, u32[]{:S(2)}) collective-permute-start(bf16[16,128,128]{2,1,0:T(8,128)(2,1)} %get-tuple-element.13.after.own), channel_id=1, source_target_pairs={{4,1},{5,2},{6,10},{8,13},{9,14},{10,6},{20,17},{21,18},{22,26},{2... | collective-permute-start | bytes 1572872 | tf_op jit(solution)/shard_map/ppermute | solution.py:376
  15.8 1.3 collective-permute-start.2
  17.1 1.9 %collective-permute-start.3 = (bf16[16,128,128]{2,1,0:T(8,128)(2,1)}, bf16[16,128,128]{2,1,0:T(8,128)(2,1)}, u32[]{:S(2)}, u32[]{:S(2)}) collective-permute-start(bf16[16,128,128]{2,1,0:T(8,128)(2,1)} %get-tuple-element.17), channel_id=1, source_target_pairs={{2,0},{6,8},{3,1},{7,9},{4,2},{0,10},{14,12},{10,4},{15,13},{11,5}... | collective-permute-start | bytes 1572872 | tf_op jit(solution)/shard_map/ppermute | solution.py:376
  19.0 1.9 %collective-permute-start.4 = (bf16[16,128,128]{2,1,0:T(8,128)(2,1)}, bf16[16,128,128]{2,1,0:T(8,128)(2,1)}, u32[]{:S(2)}, u32[]{:S(2)}) collective-permute-start(bf16[16,128,128]{2,1,0:T(8,128)(2,1)} %get-tuple-element.18), channel_id=1, source_target_pairs={{3,0},{7,8},{4,1},{0,9},{5,2},{1,10},{15,12},{11,4},{8,13},{12,5},... | collective-permute-start | bytes 1572872 | tf_op jit(solution)/shard_map/ppermute | solution.py:376
  21.0 0.0 copy-start
  21.0 5.2 %prepare.1 = (bf16[16,16,8,128]{3,2,1,0:T(8,128)(2,1)}, bf16[256,16,128]{2,1,0:T(8,128)(2,1)}, s32[2,128]{1,0:T(2,128)}) custom-call(s32[3,64]{1,0:T(4,128)} %bitcast.1, bf16[16,16,8,128]{3,2,1,0:T(8,128)(2,1)} %gradient.1, bf16[16,16,8,128]{3,2,1,0:T(8,128)(2,1)} %second.1, bf16[16,128,128]{2,1,0:T(8,128)(2,1)} %get-tuple-element.13.after.own), custom_call_target="tpu_custom_call" | custom-call | tf_op jit(solution)/shard_map/prepare/pallas_call | solution.py:167
  26.2 0.0 collective-permute-done.refs_0_
  26.2 1.3 collective-permute-start.1
  27.5 54.9 %conditional.1 = (bf16[256,16,128]{2,1,0:T(8,128)(2,1)S(1)}) conditional(s32[]{:T(128)} %convert_element_type.3, () %tuple.14, bf16[256,16,128]{2,1,0:T(8,128)(2,1)} %get-tuple-element.15.refs_1_), branch_computations={%region_0.0_spmd, %region_1.0_spmd} | conditional | bytes 2097160 | solution.py:381
  27.5 54.9 %all_to_all.9 = bf16[256,16,128]{2,1,0:T(8,128)(2,1)S(1)} all-to-all(bf16[256,16,128]{2,1,0:T(8,128)(2,1)} %param.1), channel_id=1, replica_groups=mesh['col'=32,'core'=2,'replica'=8] {'col','replica'}, dimensions={0} | all-to-all | bytes 2097152 | tf_op jit(solution)/shard_map/cond/branch_1_fun/all_to_all | solution.py:366
  82.4 0.0 collective-permute-done.2.refs_1_
  82.4 0.0 collective-permute-done.3.refs_2_
  82.4 0.0 collective-permute-done.4.refs_3_
  82.4 0.0 collective-permute-done.1.relayed
  82.5 0.0 copy-done
  82.5 1.7 %together.1.own = bf16[768,16,128]{2,1,0:T(8,128)(2,1)S(1)} custom-call(bf16[256,16,128]{2,1,0:T(8,128)(2,1)S(1)} %get-tuple-element.20.columns, bf16[16,128,128]{2,1,0:T(8,128)(2,1)S(1)} %copy-done, bf16[16,128,128]{2,1,0:T(8,128)(2,1)S(1)} %collective-permute-done.1.relayed, bf16[16,128,128]{2,1,0:T(8,128)(2,1)} %released.1.refs_0_, ...), custom_call_target="tpu_custom_call" | custom-call | tf_op jit(solution)/shard_map/together/pallas_call | solution.py:232
  84.2 0.0 copy-start.1
  84.2 0.0 copy-start.2
  84.2 5.2 %collective-permute-start.5 = (bf16[768,16,128]{2,1,0:T(8,128)(2,1)S(1)}, bf16[768,16,128]{2,1,0:T(8,128)(2,1)S(1)}, u32[]{:S(2)}, u32[]{:S(2)}) collective-permute-start(bf16[768,16,128]{2,1,0:T(8,128)(2,1)S(1)} %together.1.own), channel_id=1, source_target_pairs={{0,8},{8,0},{1,9},{9,1},{2,10},{10,2},{3,11},{11,3},{4,12},{12,4},... | collective-permute-start | bytes 9437192 | tf_op jit(solution)/shard_map/ppermute | solution.py:370
  89.4 5.3 %collective-permute-done.5.swapped = bf16[768,16,128]{2,1,0:T(8,128)(2,1)S(1)} collective-permute-done((bf16[768,16,128]{2,1,0:T(8,128)(2,1)S(1)}, bf16[768,16,128]{2,1,0:T(8,128)(2,1)S(1)}, u32[]{:S(2)}, u32[]{:S(2)}) %collective-permute-start.5) | collective-permute-done | bytes 3145760 | tf_op jit(solution)/shard_map/ppermute | solution.py:370
  94.6 6.1 %precondition.1 = bf16[256,16,128]{2,1,0:T(8,128)(2,1)S(1)} custom-call(bf16[768,16,128]{2,1,0:T(8,128)(2,1)S(1)} %together.1.own, bf16[768,16,128]{2,1,0:T(8,128)(2,1)S(1)} %collective-permute-done.5.swapped), custom_call_target="tpu_custom_call" | custom-call | flops 4294967296 | bytes 10485760 | tf_op jit(solution)/shard_map/precondition/pallas_call | solution.py:310
  100.8 47.0 %all_to_all.10.returned = bf16[256,16,128]{2,1,0:T(8,128)(2,1)S(1)} all-to-all(bf16[256,16,128]{2,1,0:T(8,128)(2,1)S(1)} %precondition.1), channel_id=1, replica_groups=mesh['col'=32,'core'=2,'replica'=8] {'col','replica'}, dimensions={0} | all-to-all | bytes 2097152 | tf_op jit(solution)/shard_map/all_to_all | solution.py:366
  147.8 0.0 copy-done.1
  147.8 0.0 copy-done.2
  147.8 2.2 %finish.1 = bf16[16,16,8,128]{3,2,1,0:T(8,128)(2,1)} custom-call(s32[2,128]{1,0:T(2,128)S(1)} %copy-done.2, bf16[256,16,128]{2,1,0:T(8,128)(2,1)S(1)} %all_to_all.10.returned, bf16[16,16,8,128]{3,2,1,0:T(8,128)(2,1)S(1)} %copy-done.1), custom_call_target="tpu_custom_call" | custom-call | tf_op jit(solution)/shard_map/finish/pallas_call | solution.py:351
  (1 shorter events, 0.0 us)
Async XLA Ops:
  3.5 22.7 %collective-permute-start = (bf16[16,128,128]{2,1,0:T(8,128)(2,1)}, bf16[16,128,128]{2,1,0:T(8,128)(2,1)}, u32[]{:S(2)}, u32[]{:S(2)}) collective-permute-start(bf16[16,128,128]{2,1,0:T(8,128)(2,1)} %get-tuple-element.13.after.own), channel_id=1, source_target_pairs={{4,1},{5,2},{6,10},{8,13},{9,14},{10,6},{20,17},{21,18},{22,26},{2... | collective-permute-start | bytes 1572872 | tf_op jit(solution)/shard_map/ppermute | solution.py:376
  15.8 66.6 %collective-permute-start.2 = (bf16[16,128,128]{2,1,0:T(8,128)(2,1)}, bf16[16,128,128]{2,1,0:T(8,128)(2,1)}, u32[]{:S(2)}, u32[]{:S(2)}) collective-permute-start(bf16[16,128,128]{2,1,0:T(8,128)(2,1)} %get-tuple-element.16), channel_id=1, source_target_pairs={{1,0},{5,8},{2,1},{6,9},{3,2},{7,10},{13,12},{9,4},{14,13},{10,5},... | collective-permute-start | bytes 1572872 | tf_op jit(solution)/shard_map/ppermute | solution.py:376
  17.1 65.3 %collective-permute-start.3 = (bf16[16,128,128]{2,1,0:T(8,128)(2,1)}, bf16[16,128,128]{2,1,0:T(8,128)(2,1)}, u32[]{:S(2)}, u32[]{:S(2)}) collective-permute-start(bf16[16,128,128]{2,1,0:T(8,128)(2,1)} %get-tuple-element.17), channel_id=1, source_target_pairs={{2,0},{6,8},{3,1},{7,9},{4,2},{0,10},{14,12},{10,4},{15,13},{11,5}... | collective-permute-start | bytes 1572872 | tf_op jit(solution)/shard_map/ppermute | solution.py:376
  19.0 63.4 %collective-permute-start.4 = (bf16[16,128,128]{2,1,0:T(8,128)(2,1)}, bf16[16,128,128]{2,1,0:T(8,128)(2,1)}, u32[]{:S(2)}, u32[]{:S(2)}) collective-permute-start(bf16[16,128,128]{2,1,0:T(8,128)(2,1)} %get-tuple-element.18), channel_id=1, source_target_pairs={{3,0},{7,8},{4,1},{0,9},{5,2},{1,10},{15,12},{11,4},{8,13},{12,5},... | collective-permute-start | bytes 1572872 | tf_op jit(solution)/shard_map/ppermute | solution.py:376
  21.0 61.5 %copy-start = (bf16[16,128,128]{2,1,0:T(8,128)(2,1)S(1)}, bf16[16,128,128]{2,1,0:T(8,128)(2,1)}, u32[]{:S(2)}) copy-start(bf16[16,128,128]{2,1,0:T(8,128)(2,1)} %get-tuple-element.13.after.own) | copy-start | bytes 1572868
  26.2 56.2 %collective-permute-start.1 = (bf16[16,128,128]{2,1,0:T(8,128)(2,1)}, bf16[16,128,128]{2,1,0:T(8,128)(2,1)S(1)}, u32[]{:S(2)}, u32[]{:S(2)}) collective-permute-start(bf16[16,128,128]{2,1,0:T(8,128)(2,1)} %released.1.refs_0_), channel_id=1, source_target_pairs={{1,8},{2,9},{13,4},{14,5},{17,24},{18,25},{29,20},{30,21},{33,40},... | collective-permute-start | bytes 1572872 | tf_op jit(solution)/shard_map/ppermute | solution.py:380
  84.2 63.6 %copy-start.1 = (bf16[16,16,8,128]{3,2,1,0:T(8,128)(2,1)S(1)}, bf16[16,16,8,128]{3,2,1,0:T(8,128)(2,1)}, u32[]{:S(2)}) copy-start(bf16[16,16,8,128]{3,2,1,0:T(8,128)(2,1)} %momentum.1) | copy-start | bytes 1572868
  84.2 63.6 %copy-start.2 = (s32[2,128]{1,0:T(2,128)S(1)}, s32[2,128]{1,0:T(2,128)}, u32[]{:S(2)}) copy-start(s32[2,128]{1,0:T(2,128)} %get-tuple-element.14.place) | copy-start | bytes 3076
  84.2 10.4 %collective-permute-start.5 = (bf16[768,16,128]{2,1,0:T(8,128)(2,1)S(1)}, bf16[768,16,128]{2,1,0:T(8,128)(2,1)S(1)}, u32[]{:S(2)}, u32[]{:S(2)}) collective-permute-start(bf16[768,16,128]{2,1,0:T(8,128)(2,1)S(1)} %together.1.own), channel_id=1, source_target_pairs={{0,8},{8,0},{1,9},{9,1},{2,10},{10,2},{3,11},{11,3},{4,12},{12,4},... | collective-permute-start | bytes 9437192 | tf_op jit(solution)/shard_map/ppermute | solution.py:370

commit v4 on v3

--- a/solution.py
+++ b/solution.py
@@ -19,6 +19,7 @@
 NOTE = 3
 CHUNKS = 4
 DIRECT = 2
+EARLY = 2
 
 ANY = pl.BlockSpec(memory_space=pl.ANY)
 HBM = pl.BlockSpec(memory_space=pltpu.HBM)
@@ -191,15 +192,17 @@
     pass
 
 
-def released(array, other):
+def released(arrays, other):
+    count = len(arrays)
     return pl.pallas_call(
         released_kernel,
-        out_shape=jax.ShapeDtypeStruct(array.shape, array.dtype),
-        in_specs=[ANY, ANY],
-        out_specs=ANY,
-        input_output_aliases={0: 0},
+        out_shape=[jax.ShapeDtypeStruct(array.shape, array.dtype) for array in arrays],
+        in_specs=[ANY] * (count + 1),
+        out_specs=[ANY] * count,
+        input_output_aliases={at: at for at in range(count)},
+        compiler_params=limit(63),
         name="released",
-    )(array, other)
+    )(*arrays, other)
 
 
 def together_kernel(columns, own, relayed, *refs):
@@ -373,10 +376,11 @@
 def local(gradient, second_moment, momentum, left_factor, right_factor, block_of_slot):
     spread = spread_factors(left_factor, right_factor)
     line = ("core", "replica")
-    factors = [lax.ppermute(shard, line, factor_pairs(step)) for step, shard in enumerate(spread)]
-
+    factors = [lax.ppermute(spread[step], line, factor_pairs(step)) for step in range(EARLY)]
     moment_new, pieces, place = prepare(block_of_slot.T, gradient, second_moment, spread[0])
-    factors[0] = released(factors[0], pieces)
+    later = released(spread[EARLY:], pieces)
+    factors += [lax.ppermute(shard, line, factor_pairs(EARLY + at)) for at, shard in enumerate(later)]
+    factors[:1] = released(factors[:1], pieces)
     relayed = lax.ppermute(factors[0], line, relay_pairs())
     columns = lax.cond(lax.axis_index("core") < CORES, exchange, jnp.zeros_like, pieces)
     held = together(columns, [spread[0], relayed] + factors)

time: 152 us -> 152 us (level)
  starting transfers between devices: 23.9 us -> 21.5 us
  blocking collectives: 102 us -> 104 us
    ppermute x1, starting transfers between devices: 5.16 us -> 2.64 us  [swap(): return lax.ppermute(array, 'core', [(0, 1), (1, 0)])]
    all_to_all x2, blocking collectives: 102 us -> 104 us  [exchange(): lax.all_to_all(array, ('col', 'replica'), split_axis=0, concat_axis=0, ti...]
where the time goes in v4:
time: 152 us; the launch traced here: 150 us
  blocking collectives  104 us (68%)
  starting transfers between devices  21.5 us (14%)
  Pallas kernels  18 us (12%)
  waiting for transfers between devices  5.28 us (3%)
    all_to_all x2, blocking collectives, exchange(): lax.all_to_all(array, ('col', 'replica'), split_axis=0, concat_axis=0, ti...  104 us
    ppermute x2, starting transfers between devices, local(): lax.ppermute(spread[step], line, factor_pairs(step))  13.6 us
    pallas_call x1, Pallas kernels, precondition(): pl.pallas_call(block_kernel, out_shape=jax.ShapeDtypeStruct((COLS * RING,...  6.08 us
    ppermute x1, waiting for transfers between devices, swap(): return lax.ppermute(array, 'core', [(0, 1), (1, 0)])  5.26 us
    pallas_call x1, Pallas kernels, prepare(): pl.pallas_call(prepare_kernel, out_shape=[jax.ShapeDtypeStruct(second.sha...  5.08 us
    ppermute x2, starting transfers between devices, local(): lax.ppermute(shard, line, factor_pairs(EARLY + at))  3.97 us
  transfers between devices with their start and end apart: 6, of which 1 were waited for; matrix products, arithmetic and copies ran while one was open for 0% of the time, Pallas kernels for 3%

profile of v4, /device:TPU:1, one launch (start us, length us, event | category | flops | bytes accessed | tf_op | source)
XLA Modules:
  0.0 149.9 jit_solution(17027358010826814050)
XLA Ops:
  0.6 2.9 %spread_factors.1 = (bf16[16,128,128]{2,1,0:T(8,128)(2,1)}, bf16[16,128,128]{2,1,0:T(8,128)(2,1)}, bf16[16,128,128]{2,1,0:T(8,128)(2,1)}, bf16[16,128,128]{2,1,0:T(8,128)(2,1)}) custom-call(bf16[3,128,1024]{2,1,0:T(8,128)(2,1)} %left.1, bf16[3,1024,128]{2,1,0:T(8,128)(2,1)} %right.1), custom_call_target="tpu_custom_call" | custom-call | tf_op jit(solution)/shard_map/spread_factors/pallas_call | solution.py:93
  3.5 12.3 %collective-permute-start = (bf16[16,128,128]{2,1,0:T(8,128)(2,1)}, bf16[16,128,128]{2,1,0:T(8,128)(2,1)}, u32[]{:S(2)}, u32[]{:S(2)}) collective-permute-start(bf16[16,128,128]{2,1,0:T(8,128)(2,1)} %get-tuple-element.15.after.own), channel_id=1, source_target_pairs={{4,1},{5,2},{6,10},{8,13},{9,14},{10,6},{20,17},{21,18},{22,26},{2... | collective-permute-start | bytes 1572872 | tf_op jit(solution)/shard_map/ppermute | solution.py:379
  15.8 1.3 collective-permute-start.2
  17.1 5.1 %prepare.1 = (bf16[16,16,8,128]{3,2,1,0:T(8,128)(2,1)}, bf16[256,16,128]{2,1,0:T(8,128)(2,1)}, s32[2,128]{1,0:T(2,128)}) custom-call(s32[3,64]{1,0:T(4,128)} %bitcast.1, bf16[16,16,8,128]{3,2,1,0:T(8,128)(2,1)} %gradient.1, bf16[16,16,8,128]{3,2,1,0:T(8,128)(2,1)} %second.1, bf16[16,128,128]{2,1,0:T(8,128)(2,1)} %get-tuple-element.15.after.own), custom_call_target="tpu_custom_call" | custom-call | tf_op jit(solution)/shard_map/prepare/pallas_call | solution.py:168
  22.2 0.0 copy-start
  22.2 2.1 %collective-permute-start.3 = (bf16[16,128,128]{2,1,0:T(8,128)(2,1)}, bf16[16,128,128]{2,1,0:T(8,128)(2,1)}, u32[]{:S(2)}, u32[]{:S(2)}) collective-permute-start(bf16[16,128,128]{2,1,0:T(8,128)(2,1)} %get-tuple-element.21), channel_id=1, source_target_pairs={{2,0},{6,8},{3,1},{7,9},{4,2},{0,10},{14,12},{10,4},{15,13},{11,5}... | collective-permute-start | bytes 1572872 | tf_op jit(solution)/shard_map/ppermute | solution.py:382
  24.3 1.9 %collective-permute-start.4 = (bf16[16,128,128]{2,1,0:T(8,128)(2,1)}, bf16[16,128,128]{2,1,0:T(8,128)(2,1)}, u32[]{:S(2)}, u32[]{:S(2)}) collective-permute-start(bf16[16,128,128]{2,1,0:T(8,128)(2,1)} %get-tuple-element.22), channel_id=1, source_target_pairs={{3,0},{7,8},{4,1},{0,9},{5,2},{1,10},{15,12},{11,4},{8,13},{12,5},... | collective-permute-start | bytes 1572872 | tf_op jit(solution)/shard_map/ppermute | solution.py:382
  26.2 0.0 collective-permute-done.refs_0_
  26.2 1.3 collective-permute-start.1
  27.5 57.4 %conditional.1 = (bf16[256,16,128]{2,1,0:T(8,128)(2,1)S(1)}) conditional(s32[]{:T(128)} %convert_element_type.3, () %tuple.14, bf16[256,16,128]{2,1,0:T(8,128)(2,1)} %get-tuple-element.17.refs_1_.refs_2_), branch_computations={%region_0.0_spmd, %region_1.0_spmd} | conditional | bytes 2097160 | solution.py:385
  27.5 57.4 %all_to_all.9 = bf16[256,16,128]{2,1,0:T(8,128)(2,1)S(1)} all-to-all(bf16[256,16,128]{2,1,0:T(8,128)(2,1)} %param.1), channel_id=1, replica_groups=mesh['col'=32,'core'=2,'replica'=8] {'col','replica'}, dimensions={0} | all-to-all | bytes 2097152 | tf_op jit(solution)/shard_map/cond/branch_1_fun/all_to_all | solution.py:369
  85.0 0.0 collective-permute-done.2.refs_1_
  85.0 0.0 collective-permute-done.3.refs_2_
  85.0 0.0 collective-permute-done.4.refs_3_
  85.0 0.0 collective-permute-done.1.relayed
  85.0 0.0 copy-done
  85.0 1.7 %together.1.own = bf16[768,16,128]{2,1,0:T(8,128)(2,1)S(1)} custom-call(bf16[256,16,128]{2,1,0:T(8,128)(2,1)S(1)} %get-tuple-element.24.columns, bf16[16,128,128]{2,1,0:T(8,128)(2,1)S(1)} %copy-done, bf16[16,128,128]{2,1,0:T(8,128)(2,1)S(1)} %collective-permute-done.1.relayed, bf16[16,128,128]{2,1,0:T(8,128)(2,1)} %released.2.refs_0_, ...), custom_call_target="tpu_custom_call" | custom-call | tf_op jit(solution)/shard_map/together/pallas_call | solution.py:235
  86.7 0.0 copy-start.1
  86.7 0.0 copy-start.2
  86.7 2.6 %collective-permute-start.5 = (bf16[768,16,128]{2,1,0:T(8,128)(2,1)S(1)}, bf16[768,16,128]{2,1,0:T(8,128)(2,1)S(1)}, u32[]{:S(2)}, u32[]{:S(2)}) collective-permute-start(bf16[768,16,128]{2,1,0:T(8,128)(2,1)S(1)} %together.1.own), channel_id=1, source_target_pairs={{0,8},{8,0},{1,9},{9,1},{2,10},{10,2},{3,11},{11,3},{4,12},{12,4},... | collective-permute-start | bytes 9437192 | tf_op jit(solution)/shard_map/ppermute | solution.py:373
  89.4 5.3 %collective-permute-done.5.swapped = bf16[768,16,128]{2,1,0:T(8,128)(2,1)S(1)} collective-permute-done((bf16[768,16,128]{2,1,0:T(8,128)(2,1)S(1)}, bf16[768,16,128]{2,1,0:T(8,128)(2,1)S(1)}, u32[]{:S(2)}, u32[]{:S(2)}) %collective-permute-start.5) | collective-permute-done | bytes 3145760 | tf_op jit(solution)/shard_map/ppermute | solution.py:373
  94.7 6.1 %precondition.1 = bf16[256,16,128]{2,1,0:T(8,128)(2,1)S(1)} custom-call(bf16[768,16,128]{2,1,0:T(8,128)(2,1)S(1)} %together.1.own, bf16[768,16,128]{2,1,0:T(8,128)(2,1)S(1)} %collective-permute-done.5.swapped), custom_call_target="tpu_custom_call" | custom-call | flops 4294967296 | bytes 10485760 | tf_op jit(solution)/shard_map/precondition/pallas_call | solution.py:313
  100.7 47.0 %all_to_all.10.returned = bf16[256,16,128]{2,1,0:T(8,128)(2,1)S(1)} all-to-all(bf16[256,16,128]{2,1,0:T(8,128)(2,1)S(1)} %precondition.1), channel_id=1, replica_groups=mesh['col'=32,'core'=2,'replica'=8] {'col','replica'}, dimensions={0} | all-to-all | bytes 2097152 | tf_op jit(solution)/shard_map/all_to_all | solution.py:369
  147.7 0.0 copy-done.1
  147.7 0.0 copy-done.2
  147.7 2.2 %finish.1 = bf16[16,16,8,128]{3,2,1,0:T(8,128)(2,1)} custom-call(s32[2,128]{1,0:T(2,128)S(1)} %copy-done.2, bf16[256,16,128]{2,1,0:T(8,128)(2,1)S(1)} %all_to_all.10.returned, bf16[16,16,8,128]{3,2,1,0:T(8,128)(2,1)S(1)} %copy-done.1), custom_call_target="tpu_custom_call" | custom-call | tf_op jit(solution)/shard_map/finish/pallas_call | solution.py:354
  (2 shorter events, 0.0 us)
Async XLA Ops:
  3.5 22.7 %collective-permute-start = (bf16[16,128,128]{2,1,0:T(8,128)(2,1)}, bf16[16,128,128]{2,1,0:T(8,128)(2,1)}, u32[]{:S(2)}, u32[]{:S(2)}) collective-permute-start(bf16[16,128,128]{2,1,0:T(8,128)(2,1)} %get-tuple-element.15.after.own), channel_id=1, source_target_pairs={{4,1},{5,2},{6,10},{8,13},{9,14},{10,6},{20,17},{21,18},{22,26},{2... | collective-permute-start | bytes 1572872 | tf_op jit(solution)/shard_map/ppermute | solution.py:379
  15.8 69.1 %collective-permute-start.2 = (bf16[16,128,128]{2,1,0:T(8,128)(2,1)}, bf16[16,128,128]{2,1,0:T(8,128)(2,1)}, u32[]{:S(2)}, u32[]{:S(2)}) collective-permute-start(bf16[16,128,128]{2,1,0:T(8,128)(2,1)} %get-tuple-element.18), channel_id=1, source_target_pairs={{1,0},{5,8},{2,1},{6,9},{3,2},{7,10},{13,12},{9,4},{14,13},{10,5},... | collective-permute-start | bytes 1572872 | tf_op jit(solution)/shard_map/ppermute | solution.py:379
  22.2 62.8 %copy-start = (bf16[16,128,128]{2,1,0:T(8,128)(2,1)S(1)}, bf16[16,128,128]{2,1,0:T(8,128)(2,1)}, u32[]{:S(2)}) copy-start(bf16[16,128,128]{2,1,0:T(8,128)(2,1)} %get-tuple-element.15.after.own) | copy-start | bytes 1572868
  22.2 62.7 %collective-permute-start.3 = (bf16[16,128,128]{2,1,0:T(8,128)(2,1)}, bf16[16,128,128]{2,1,0:T(8,128)(2,1)}, u32[]{:S(2)}, u32[]{:S(2)}) collective-permute-start(bf16[16,128,128]{2,1,0:T(8,128)(2,1)} %get-tuple-element.21), channel_id=1, source_target_pairs={{2,0},{6,8},{3,1},{7,9},{4,2},{0,10},{14,12},{10,4},{15,13},{11,5}... | collective-permute-start | bytes 1572872 | tf_op jit(solution)/shard_map/ppermute | solution.py:382
  24.3 60.7 %collective-permute-start.4 = (bf16[16,128,128]{2,1,0:T(8,128)(2,1)}, bf16[16,128,128]{2,1,0:T(8,128)(2,1)}, u32[]{:S(2)}, u32[]{:S(2)}) collective-permute-start(bf16[16,128,128]{2,1,0:T(8,128)(2,1)} %get-tuple-element.22), channel_id=1, source_target_pairs={{3,0},{7,8},{4,1},{0,9},{5,2},{1,10},{15,12},{11,4},{8,13},{12,5},... | collective-permute-start | bytes 1572872 | tf_op jit(solution)/shard_map/ppermute | solution.py:382
  26.2 58.7 %collective-permute-start.1 = (bf16[16,128,128]{2,1,0:T(8,128)(2,1)}, bf16[16,128,128]{2,1,0:T(8,128)(2,1)S(1)}, u32[]{:S(2)}, u32[]{:S(2)}) collective-permute-start(bf16[16,128,128]{2,1,0:T(8,128)(2,1)} %released.2.refs_0_), channel_id=1, source_target_pairs={{1,8},{2,9},{13,4},{14,5},{17,24},{18,25},{29,20},{30,21},{33,40},... | collective-permute-start | bytes 1572872 | tf_op jit(solution)/shard_map/ppermute | solution.py:384
  86.7 61.0 %copy-start.1 = (bf16[16,16,8,128]{3,2,1,0:T(8,128)(2,1)S(1)}, bf16[16,16,8,128]{3,2,1,0:T(8,128)(2,1)}, u32[]{:S(2)}) copy-start(bf16[16,16,8,128]{3,2,1,0:T(8,128)(2,1)} %momentum.1) | copy-start | bytes 1572868
  86.7 61.0 %copy-start.2 = (s32[2,128]{1,0:T(2,128)S(1)}, s32[2,128]{1,0:T(2,128)}, u32[]{:S(2)}) copy-start(s32[2,128]{1,0:T(2,128)} %get-tuple-element.16.place) | copy-start | bytes 3076
  86.7 7.9 %collective-permute-start.5 = (bf16[768,16,128]{2,1,0:T(8,128)(2,1)S(1)}, bf16[768,16,128]{2,1,0:T(8,128)(2,1)S(1)}, u32[]{:S(2)}, u32[]{:S(2)}) collective-permute-start(bf16[768,16,128]{2,1,0:T(8,128)(2,1)S(1)} %together.1.own), channel_id=1, source_target_pairs={{0,8},{8,0},{1,9},{9,1},{2,10},{10,2},{3,11},{11,3},{4,12},{12,4},... | collective-permute-start | bytes 9437192 | tf_op jit(solution)/shard_map/ppermute | solution.py:373

commit v5 on v3

--- a/solution.py
+++ b/solution.py
@@ -65,17 +65,32 @@
     return pairs
 
 
-def factor_kernel(left, right, *refs):
-    outs, held_left, held_right, sems = refs[:PLACES], *refs[PLACES:]
+def prepare_kernel(slots, gradient, second, left, right, moment, pieces_out, place, *rest):
+    spread_out, held_gradient, held_second, held_moment = rest[:PLACES], *rest[PLACES : PLACES + 3]
+    held_left, held_right, spread, pieces, wide, square, notes, sems, factor_sems = rest[PLACES + 3 :]
+    block_rows, shard_rows, block_cols, lanes = gradient.shape
     part = left.shape[1]
+    per_row = shard_rows * block_cols
+    chunk = block_rows // CHUNKS
+    factor_in, first, second_in, moment_copies, piece_copies = [], [], [], [], []
+    for s in range(SLOTS):
+        factor_in.append(pltpu.make_async_copy(left.at[s], held_left.at[s], factor_sems.at[0, s]))
+        factor_in.append(pltpu.make_async_copy(right.at[s], held_right.at[s], factor_sems.at[1, s]))
+    for at in range(CHUNKS):
+        rows = pl.ds(at * chunk, chunk)
+        first.append(pltpu.make_async_copy(gradient.at[rows], held_gradient.at[rows], sems.at[0, at]))
+        second_in.append(pltpu.make_async_copy(second.at[rows], held_second.at[rows], sems.at[1, at]))
+        moment_copies.append(pltpu.make_async_copy(held_moment.at[rows], moment.at[rows], sems.at[2, at]))
+        group = pl.ds(at * (COLS * RING // CHUNKS), COLS * RING // CHUNKS)
+        piece_copies.append(pltpu.make_async_copy(pieces.at[group], pieces_out.at[group], sems.at[3, at]))
+    for copy in factor_in + first + second_in:
+        copy.start()
+
+    spread_copies = [
+        pltpu.make_async_copy(spread.at[step], spread_out[step], factor_sems.at[2, step]) for step in range(PLACES)
+    ]
     here = lax.axis_index("replica")
-    copies = []
-    for s in range(SLOTS):
-        copies.append(pltpu.make_async_copy(left.at[s], held_left.at[s], sems.at[0, s]))
-        copies.append(pltpu.make_async_copy(right.at[s], held_right.at[s], sems.at[1, s]))
-    for copy in copies:
-        copy.start()
-    for copy in copies:
+    for copy in factor_in:
         copy.wait()
     for step in range(PLACES):
         slot = lax.rem(here - step + RING, PLACES)
@@ -83,40 +98,9 @@
         @pl.when(slot < SLOTS)
         def _():
             for j in range(RING):
-                outs[step][j] = held_left[slot, :, j * part : (j + 1) * part]
-                outs[step][RING + j] = held_right[slot, j * part : (j + 1) * part, :]
-
-
-def spread_factors(left, right):
-    part = left.shape[1]
-    return pl.pallas_call(
-        factor_kernel,
-        out_shape=[jax.ShapeDtypeStruct((2 * RING, part, part), left.dtype)] * PLACES,
-        in_specs=[HBM, HBM],
-        out_specs=[VMEM] * PLACES,
-        scratch_shapes=[
-            pltpu.VMEM(left.shape, left.dtype),
-            pltpu.VMEM(right.shape, right.dtype),
-            pltpu.SemaphoreType.DMA((2, SLOTS)),
-        ],
-        compiler_params=limit(63),
-        name="spread_factors",
-    )(left, right)
-
-
-def prepare_kernel(slots, gradient, second, after, moment, pieces, place, *scratch):
-    held_gradient, held_second, held_moment, wide, square, notes, sems = scratch
-    block_rows, shard_rows, block_cols, lanes = gradient.shape
-    per_row = shard_rows * block_cols
-    chunk = block_rows // CHUNKS
-    chunks = [pl.ds(at * chunk, chunk) for at in range(CHUNKS)]
-    first, second_in, out = [], [], []
-    for at, rows in enumerate(chunks):
-        first.append(pltpu.make_async_copy(gradient.at[rows], held_gradient.at[rows], sems.at[0, at]))
-        second_in.append(pltpu.make_async_copy(second.at[rows], held_second.at[rows], sems.at[1, at]))
-        out.append(pltpu.make_async_copy(held_moment.at[rows], moment.at[rows], sems.at[2, at]))
-        first[at].start()
-        second_in[at].start()
+                spread[step, j] = held_left[slot, :, j * part : (j + 1) * part]
+                spread[step, RING + j] = held_right[slot, j * part : (j + 1) * part, :]
+            spread_copies[step].start()
 
     def adam(i, carry):
         g = held_gradient[i].astype(jnp.float32)
@@ -131,7 +115,7 @@
         first[at].wait()
         second_in[at].wait()
         lax.fori_loop(at * chunk, (at + 1) * chunk, adam, 0)
-        out[at].start()
+        moment_copies[at].start()
     notes[...] = jnp.zeros(notes.shape, notes.dtype)
 
     def column(col, carry):
@@ -156,50 +140,53 @@
         pieces[member(col, NOTE)] = notes[...].astype(pieces.dtype)
         return carry
 
-    lax.fori_loop(0, COLS, column, 0)
-    for copy in out:
+    for at in range(CHUNKS):
+        lax.fori_loop(at * (COLS // CHUNKS), (at + 1) * (COLS // CHUNKS), column, 0)
+        piece_copies[at].start()
+    for step in range(PLACES):
+        slot = lax.rem(here - step + RING, PLACES)
+
+        @pl.when(slot < SLOTS)
+        def _():
+            spread_copies[step].wait()
+
+    for copy in moment_copies + piece_copies:
         copy.wait()
 
 
-def prepare(slots, gradient, second, after):
+def prepare(slots, gradient, second, left, right):
     block_rows, shard_rows, block_cols, lanes = gradient.shape
     block_count = block_rows * block_cols
+    part = left.shape[1]
+    kind = gradient.dtype
+    dma = pltpu.SemaphoreType.DMA
     return pl.pallas_call(
         prepare_kernel,
         out_shape=[
             jax.ShapeDtypeStruct(second.shape, second.dtype),
-            jax.ShapeDtypeStruct((COLS * RING, shard_rows, lanes), gradient.dtype),
+            jax.ShapeDtypeStruct((COLS * RING, shard_rows, lanes), kind),
             jax.ShapeDtypeStruct((2, block_count), jnp.int32),
-        ],
-        in_specs=[SMEM, HBM, HBM, ANY],
-        out_specs=[HBM, VMEM, SMEM],
+        ]
+        + [jax.ShapeDtypeStruct((2 * RING, part, part), left.dtype)] * PLACES,
+        in_specs=[SMEM] + [HBM] * 4,
+        out_specs=[HBM, HBM, SMEM] + [HBM] * PLACES,
         scratch_shapes=[
-            pltpu.VMEM(gradient.shape, gradient.dtype),
+            pltpu.VMEM(gradient.shape, kind),
             pltpu.VMEM(second.shape, second.dtype),
             pltpu.VMEM(second.shape, second.dtype),
+            pltpu.VMEM(left.shape, left.dtype),
+            pltpu.VMEM(right.shape, right.dtype),
+            pltpu.VMEM((PLACES, 2 * RING, part, part), left.dtype),
+            pltpu.VMEM((COLS * RING, shard_rows, lanes), kind),
             pltpu.VMEM((block_count * shard_rows, lanes), jnp.float32),
             pltpu.VMEM((block_count, lanes), jnp.float32),
             pltpu.VMEM((shard_rows, lanes), jnp.float32),
-            pltpu.SemaphoreType.DMA((3, CHUNKS)),
+            dma((4, CHUNKS)),
+            dma((3, PLACES)),
         ],
         compiler_params=limit(63),
         name="prepare",
-    )(slots, gradient, second, after)
-
-
-def released_kernel(*refs):
-    pass
-
-
-def released(array, other):
-    return pl.pallas_call(
-        released_kernel,
-        out_shape=jax.ShapeDtypeStruct(array.shape, array.dtype),
-        in_specs=[ANY, ANY],
-        out_specs=ANY,
-        input_output_aliases={0: 0},
-        name="released",
-    )(array, other)
+    )(slots, gradient, second, left, right)
 
 
 def together_kernel(columns, own, relayed, *refs):
@@ -371,12 +358,11 @@
 
 
 def local(gradient, second_moment, momentum, left_factor, right_factor, block_of_slot):
-    spread = spread_factors(left_factor, right_factor)
+    moment_new, pieces, place, *spread = prepare(
+        block_of_slot.T, gradient, second_moment, left_factor, right_factor
+    )
     line = ("core", "replica")
     factors = [lax.ppermute(shard, line, factor_pairs(step)) for step, shard in enumerate(spread)]
-
-    moment_new, pieces, place = prepare(block_of_slot.T, gradient, second_moment, spread[0])
-    factors[0] = released(factors[0], pieces)
     relayed = lax.ppermute(factors[0], line, relay_pairs())
     columns = lax.cond(lax.axis_index("core") < CORES, exchange, jnp.zeros_like, pieces)
     held = together(columns, [spread[0], relayed] + factors)

time: 152 us -> 155 us (1.020)
  waiting for transfers between devices: 5.28 us -> 9.27 us
  starting transfers between devices: 23.9 us -> 26.1 us
  Pallas kernels: 18.2 us -> 16.1 us
    ppermute x4, waiting for transfers between devices: 0.01 us -> 4.01 us  [local(): lax.ppermute(shard, line, factor_pairs(step))]
    pallas_call x2 -> x0, Pallas kernels: 2.9 us -> none  [the longest x1 2.9 us: spread_factors(): pl.pallas_call(factor_kernel, out_shape=[jax.ShapeDtypeStruct((2 * RING,...]
    ppermute x1, starting transfers between devices: 5.16 us -> 7.79 us  [swap(): return lax.ppermute(array, 'core', [(0, 1), (1, 0)])]
  transfers between devices with their start and end apart: 6 -> 6, of which waited for: 1 -> 2; matrix products, arithmetic and copies ran while one was open for 0% -> 0% of each run, Pallas kernels for 3% -> 0%
where the time goes in v5:
time: 155 us; the launch traced here: 153 us
  blocking collectives  101 us (65%)
  starting transfers between devices  26.1 us (17%)
  Pallas kernels  16.1 us (10%)
  waiting for transfers between devices  9.27 us (6%)
    all_to_all x2, blocking collectives, exchange(): lax.all_to_all(array, ('col', 'replica'), split_axis=0, concat_axis=0, ti...  101 us
    ppermute x4, starting transfers between devices, local(): lax.ppermute(shard, line, factor_pairs(step))  17 us
    ppermute x1, starting transfers between devices, swap(): return lax.ppermute(array, 'core', [(0, 1), (1, 0)])  7.79 us
    pallas_call x1, Pallas kernels, prepare(): pl.pallas_call(prepare_kernel, out_shape=[jax.ShapeDtypeStruct(second.sha...  6.41 us
    pallas_call x1, Pallas kernels, precondition(): pl.pallas_call(block_kernel, out_shape=jax.ShapeDtypeStruct((COLS * RING,...  6.08 us
    ppermute x1, waiting for transfers between devices, swap(): return lax.ppermute(array, 'core', [(0, 1), (1, 0)])  5.26 us
    ppermute x4, waiting for transfers between devices, local(): lax.ppermute(shard, line, factor_pairs(step))  4.01 us
  transfers between devices with their start and end apart: 6, of which 2 were waited for; matrix products, arithmetic and copies ran while one was open for 0% of the time, Pallas kernels for 0%

profile of v5, /device:TPU:1, one launch (start us, length us, event | category | flops | bytes accessed | tf_op | source)
XLA Modules:
  0.0 153.4 jit_solution(15213993476360157642)
XLA Ops:
  0.6 6.4 %prepare.1 = (bf16[16,16,8,128]{3,2,1,0:T(8,128)(2,1)}, bf16[256,16,128]{2,1,0:T(8,128)(2,1)}, s32[2,128]{1,0:T(2,128)}, bf16[16,128,128]{2,1,0:T(8,128)(2,1)}, ...) custom-call(s32[3,64]{1,0:T(4,128)} %bitcast.1, ...), custom_call_target="tpu_custom_call" | custom-call | tf_op jit(solution)/shard_map/prepare/pallas_call | solution.py:163
  7.0 0.0 copy-start
  7.1 11.6 %collective-permute-start = (bf16[16,128,128]{2,1,0:T(8,128)(2,1)}, bf16[16,128,128]{2,1,0:T(8,128)(2,1)S(1)}, u32[]{:S(2)}, u32[]{:S(2)}) collective-permute-start(bf16[16,128,128]{2,1,0:T(8,128)(2,1)} %get-tuple-element.15.own), channel_id=1, source_target_pairs={{4,1},{5,2},{6,10},{8,13},{9,14},{10,6},{20,17},{21,18},{22,26},{2... | collective-permute-start | bytes 1572872 | tf_op jit(solution)/shard_map/ppermute | solution.py:365
  18.7 1.3 collective-permute-start.2
  20.0 2.2 %collective-permute-start.3 = (bf16[16,128,128]{2,1,0:T(8,128)(2,1)}, bf16[16,128,128]{2,1,0:T(8,128)(2,1)S(1)}, u32[]{:S(2)}, u32[]{:S(2)}) collective-permute-start(bf16[16,128,128]{2,1,0:T(8,128)(2,1)} %get-tuple-element.17), channel_id=1, source_target_pairs={{2,0},{6,8},{3,1},{7,9},{4,2},{0,10},{14,12},{10,4},{15,13},{11,5}... | collective-permute-start | bytes 1572872 | tf_op jit(solution)/shard_map/ppermute | solution.py:365
  22.2 1.9 %collective-permute-start.4 = (bf16[16,128,128]{2,1,0:T(8,128)(2,1)}, bf16[16,128,128]{2,1,0:T(8,128)(2,1)S(1)}, u32[]{:S(2)}, u32[]{:S(2)}) collective-permute-start(bf16[16,128,128]{2,1,0:T(8,128)(2,1)} %get-tuple-element.18), channel_id=1, source_target_pairs={{3,0},{7,8},{4,1},{0,9},{5,2},{1,10},{15,12},{11,4},{8,13},{12,5},... | collective-permute-start | bytes 1572872 | tf_op jit(solution)/shard_map/ppermute | solution.py:365
  24.1 4.0 %collective-permute-done.refs_0_ = bf16[16,128,128]{2,1,0:T(8,128)(2,1)S(1)} collective-permute-done((bf16[16,128,128]{2,1,0:T(8,128)(2,1)}, bf16[16,128,128]{2,1,0:T(8,128)(2,1)S(1)}, u32[]{:S(2)}, u32[]{:S(2)}) %collective-permute-start) | collective-permute-done | bytes 524320 | tf_op jit(solution)/shard_map/ppermute | solution.py:365
  28.1 1.3 collective-permute-start.1
  29.4 54.2 %conditional.1 = (bf16[256,16,128]{2,1,0:T(8,128)(2,1)}) conditional(s32[]{:T(128)} %convert_element_type.3, () %tuple.14, bf16[256,16,128]{2,1,0:T(8,128)(2,1)} %get-tuple-element.14), branch_computations={%region_0.0_spmd, %region_1.0_spmd} | conditional | bytes 2097160 | solution.py:367
  29.4 54.2 %all_to_all.9 = bf16[256,16,128]{2,1,0:T(8,128)(2,1)} all-to-all(bf16[256,16,128]{2,1,0:T(8,128)(2,1)} %param.1), channel_id=1, replica_groups=mesh['col'=32,'core'=2,'replica'=8] {'col','replica'}, dimensions={0} | all-to-all | bytes 2097152 | tf_op jit(solution)/shard_map/cond/branch_1_fun/all_to_all | solution.py:353
  83.6 0.0 collective-permute-done.2.refs_1_
  83.6 0.0 collective-permute-done.3.refs_2_
  83.6 0.0 collective-permute-done.4.refs_3_
  83.6 0.0 collective-permute-done.1.relayed
  83.6 0.0 copy-done
  83.6 1.4 together.1.own
  85.1 0.0 copy-start.1
  85.1 0.0 copy-start.2
  85.1 7.8 %collective-permute-start.5 = (bf16[768,16,128]{2,1,0:T(8,128)(2,1)S(1)}, bf16[768,16,128]{2,1,0:T(8,128)(2,1)S(1)}, u32[]{:S(2)}, u32[]{:S(2)}) collective-permute-start(bf16[768,16,128]{2,1,0:T(8,128)(2,1)S(1)} %together.1.own), channel_id=1, source_target_pairs={{0,8},{8,0},{1,9},{9,1},{2,10},{10,2},{3,11},{11,3},{4,12},{12,4},... | collective-permute-start | bytes 9437192 | tf_op jit(solution)/shard_map/ppermute | solution.py:357
  92.9 5.3 %collective-permute-done.5.swapped = bf16[768,16,128]{2,1,0:T(8,128)(2,1)S(1)} collective-permute-done((bf16[768,16,128]{2,1,0:T(8,128)(2,1)S(1)}, bf16[768,16,128]{2,1,0:T(8,128)(2,1)S(1)}, u32[]{:S(2)}, u32[]{:S(2)}) %collective-permute-start.5) | collective-permute-done | bytes 3145760 | tf_op jit(solution)/shard_map/ppermute | solution.py:357
  98.2 6.1 %precondition.1 = bf16[256,16,128]{2,1,0:T(8,128)(2,1)S(1)} custom-call(bf16[768,16,128]{2,1,0:T(8,128)(2,1)S(1)} %together.1.own, bf16[768,16,128]{2,1,0:T(8,128)(2,1)S(1)} %collective-permute-done.5.swapped), custom_call_target="tpu_custom_call" | custom-call | flops 4294967296 | bytes 10485760 | tf_op jit(solution)/shard_map/precondition/pallas_call | solution.py:297
  104.2 46.9 %all_to_all.10.returned = bf16[256,16,128]{2,1,0:T(8,128)(2,1)S(1)} all-to-all(bf16[256,16,128]{2,1,0:T(8,128)(2,1)S(1)} %precondition.1), channel_id=1, replica_groups=mesh['col'=32,'core'=2,'replica'=8] {'col','replica'}, dimensions={0} | all-to-all | bytes 2097152 | tf_op jit(solution)/shard_map/all_to_all | solution.py:353
  151.2 0.0 copy-done.1
  151.2 0.0 copy-done.2
  151.2 2.2 %finish.1 = bf16[16,16,8,128]{3,2,1,0:T(8,128)(2,1)} custom-call(s32[2,128]{1,0:T(2,128)S(1)} %copy-done.2, bf16[256,16,128]{2,1,0:T(8,128)(2,1)S(1)} %all_to_all.10.returned, bf16[16,16,8,128]{3,2,1,0:T(8,128)(2,1)S(1)} %copy-done.1), custom_call_target="tpu_custom_call" | custom-call | tf_op jit(solution)/shard_map/finish/pallas_call | solution.py:338
Async XLA Ops:
  7.0 76.6 %copy-start = (bf16[16,128,128]{2,1,0:T(8,128)(2,1)S(1)}, bf16[16,128,128]{2,1,0:T(8,128)(2,1)}, u32[]{:S(2)}) copy-start(bf16[16,128,128]{2,1,0:T(8,128)(2,1)} %get-tuple-element.15.own) | copy-start | bytes 1572868
  7.1 21.0 %collective-permute-start = (bf16[16,128,128]{2,1,0:T(8,128)(2,1)}, bf16[16,128,128]{2,1,0:T(8,128)(2,1)S(1)}, u32[]{:S(2)}, u32[]{:S(2)}) collective-permute-start(bf16[16,128,128]{2,1,0:T(8,128)(2,1)} %get-tuple-element.15.own), channel_id=1, source_target_pairs={{4,1},{5,2},{6,10},{8,13},{9,14},{10,6},{20,17},{21,18},{22,26},{2... | collective-permute-start | bytes 1572872 | tf_op jit(solution)/shard_map/ppermute | solution.py:365
  18.7 64.9 %collective-permute-start.2 = (bf16[16,128,128]{2,1,0:T(8,128)(2,1)}, bf16[16,128,128]{2,1,0:T(8,128)(2,1)S(1)}, u32[]{:S(2)}, u32[]{:S(2)}) collective-permute-start(bf16[16,128,128]{2,1,0:T(8,128)(2,1)} %get-tuple-element.16), channel_id=1, source_target_pairs={{1,0},{5,8},{2,1},{6,9},{3,2},{7,10},{13,12},{9,4},{14,13},{10,5},... | collective-permute-start | bytes 1572872 | tf_op jit(solution)/shard_map/ppermute | solution.py:365
  20.0 63.6 %collective-permute-start.3 = (bf16[16,128,128]{2,1,0:T(8,128)(2,1)}, bf16[16,128,128]{2,1,0:T(8,128)(2,1)S(1)}, u32[]{:S(2)}, u32[]{:S(2)}) collective-permute-start(bf16[16,128,128]{2,1,0:T(8,128)(2,1)} %get-tuple-element.17), channel_id=1, source_target_pairs={{2,0},{6,8},{3,1},{7,9},{4,2},{0,10},{14,12},{10,4},{15,13},{11,5}... | collective-permute-start | bytes 1572872 | tf_op jit(solution)/shard_map/ppermute | solution.py:365
  22.2 61.4 %collective-permute-start.4 = (bf16[16,128,128]{2,1,0:T(8,128)(2,1)}, bf16[16,128,128]{2,1,0:T(8,128)(2,1)S(1)}, u32[]{:S(2)}, u32[]{:S(2)}) collective-permute-start(bf16[16,128,128]{2,1,0:T(8,128)(2,1)} %get-tuple-element.18), channel_id=1, source_target_pairs={{3,0},{7,8},{4,1},{0,9},{5,2},{1,10},{15,12},{11,4},{8,13},{12,5},... | collective-permute-start | bytes 1572872 | tf_op jit(solution)/shard_map/ppermute | solution.py:365
  28.1 55.5 %collective-permute-start.1 = (bf16[16,128,128]{2,1,0:T(8,128)(2,1)S(1)}, bf16[16,128,128]{2,1,0:T(8,128)(2,1)S(1)}, u32[]{:S(2)}, u32[]{:S(2)}) collective-permute-start(bf16[16,128,128]{2,1,0:T(8,128)(2,1)S(1)} %collective-permute-done.refs_0_), channel_id=1, source_target_pairs={{1,8},{2,9},{13,4},{14,5},{17,24},{18,25},{29,20},{30,21},{33,40},... | collective-permute-start | bytes 1572872 | tf_op jit(solution)/shard_map/ppermute | solution.py:366
  85.1 66.1 %copy-start.1 = (bf16[16,16,8,128]{3,2,1,0:T(8,128)(2,1)S(1)}, bf16[16,16,8,128]{3,2,1,0:T(8,128)(2,1)}, u32[]{:S(2)}) copy-start(bf16[16,16,8,128]{3,2,1,0:T(8,128)(2,1)} %momentum.1) | copy-start | bytes 1572868
  85.1 66.1 %copy-start.2 = (s32[2,128]{1,0:T(2,128)S(1)}, s32[2,128]{1,0:T(2,128)}, u32[]{:S(2)}) copy-start(s32[2,128]{1,0:T(2,128)} %get-tuple-element.13.place) | copy-start | bytes 3076
  85.1 13.1 %collective-permute-start.5 = (bf16[768,16,128]{2,1,0:T(8,128)(2,1)S(1)}, bf16[768,16,128]{2,1,0:T(8,128)(2,1)S(1)}, u32[]{:S(2)}, u32[]{:S(2)}) collective-permute-start(bf16[768,16,128]{2,1,0:T(8,128)(2,1)S(1)} %together.1.own), channel_id=1, source_target_pairs={{0,8},{8,0},{1,9},{9,1},{2,10},{10,2},{3,11},{11,3},{4,12},{12,4},... | collective-permute-start | bytes 9437192 | tf_op jit(solution)/shard_map/ppermute | solution.py:357

commit v6 on v4

--- a/solution.py
+++ b/solution.py
@@ -18,7 +18,8 @@
 CORES = 2
 NOTE = 3
 CHUNKS = 4
-DIRECT = 2
+RELAYED = (1, 0)
+BESIDE = (-1, 1)
 EARLY = 2
 
 ANY = pl.BlockSpec(memory_space=pl.ANY)
@@ -49,25 +50,23 @@
             if step > 0:
                 pairs.append((c * RING + near, c * RING + root))
                 pairs.append((c * RING + far, (1 - c) * RING + root))
-            elif s == DIRECT:
+            elif s == RELAYED[c]:
+                pairs.append((c * RING + far, c * RING + (root + BESIDE[c]) % RING))
+            else:
                 pairs.append((c * RING + far, (1 - c) * RING + root))
-            else:
-                pairs.append((c * RING + far, c * RING + root + 1))
     return pairs
 
 
 def relay_pairs():
     pairs = []
     for c in range(CORES):
-        for s in range(SLOTS):
-            root = PLACES * c + s
-            if s != DIRECT:
-                pairs.append((c * RING + root + 1, (1 - c) * RING + root))
+        root = PLACES * c + RELAYED[c]
+        pairs.append((c * RING + (root + BESIDE[c]) % RING, (1 - c) * RING + root))
     return pairs
 
 
 def factor_kernel(left, right, *refs):
-    outs, held_left, held_right, sems = refs[:PLACES], *refs[PLACES:]
+    outs, held_left, held_right, spread, sems = refs[:PLACES], *refs[PLACES:]
     part = left.shape[1]
     here = lax.axis_index("replica")
     copies = []
@@ -78,27 +77,38 @@
         copy.start()
     for copy in copies:
         copy.wait()
+    out_copies = [pltpu.make_async_copy(spread.at[step], outs[step], sems.at[2, step]) for step in range(PLACES)]
     for step in range(PLACES):
         slot = lax.rem(here - step + RING, PLACES)
 
         @pl.when(slot < SLOTS)
         def _():
             for j in range(RING):
-                outs[step][j] = held_left[slot, :, j * part : (j + 1) * part]
-                outs[step][RING + j] = held_right[slot, j * part : (j + 1) * part, :]
+                spread[step, j] = held_left[slot, :, j * part : (j + 1) * part]
+                spread[step, RING + j] = held_right[slot, j * part : (j + 1) * part, :]
+            out_copies[step].start()
+
+    for step in range(PLACES):
+        slot = lax.rem(here - step + RING, PLACES)
+
+        @pl.when(slot < SLOTS)
+        def _():
+            out_copies[step].wait()
 
 
 def spread_factors(left, right):
     part = left.shape[1]
+    shape = (2 * RING, part, part)
     return pl.pallas_call(
         factor_kernel,
-        out_shape=[jax.ShapeDtypeStruct((2 * RING, part, part), left.dtype)] * PLACES,
+        out_shape=[jax.ShapeDtypeStruct(shape, left.dtype)] * PLACES,
         in_specs=[HBM, HBM],
-        out_specs=[VMEM] * PLACES,
+        out_specs=[HBM] * PLACES,
         scratch_shapes=[
             pltpu.VMEM(left.shape, left.dtype),
             pltpu.VMEM(right.shape, right.dtype),
-            pltpu.SemaphoreType.DMA((2, SLOTS)),
+            pltpu.VMEM((PLACES,) + shape, left.dtype),
+            pltpu.SemaphoreType.DMA((3, PLACES)),
         ],
         compiler_params=limit(63),
         name="spread_factors",
@@ -211,7 +221,8 @@
     size = own.shape[0] * own.shape[1] // rows
     here = lax.axis_index("replica")
     at_home = lax.div(here, PLACES) == lax.axis_index("core")
-    direct = lax.rem(here, PLACES) == DIRECT
+    slot = lax.rem(here, PLACES)
+    direct = slot != jnp.where(here < PLACES, RELAYED[0], RELAYED[1])
     out[:count] = columns[...]
     for step in range(1, PLACES):
         out[count + step * size : count + (step + 1) * size] = factors[step][...].reshape(size, rows, part)
@@ -346,7 +357,7 @@
         out[i] = (BETA_ONE * momentum[i].astype(jnp.float32) + grafted).astype(out.dtype)
         return carry
 
-    lax.fori_loop(0, block_rows, step, 0)
+    lax.fori_loop(0, block_rows, step, 0, unroll=2)
 
 
 def finish(place, returned, momentum):

time: 152 us -> 155 us (1.020)
  waiting for transfers between devices: 5.28 us -> 9.89 us
  blocking collectives: 104 us -> 101 us
  starting transfers between devices: 21.5 us -> 23.2 us
    ppermute x2, waiting for transfers between devices: 0.01 us -> 4.62 us  [local(): lax.ppermute(shard, line, factor_pairs(EARLY + at))]
    all_to_all x2, blocking collectives: 104 us -> 101 us  [exchange(): lax.all_to_all(array, ('col', 'replica'), split_axis=0, concat_axis=0, ti...]
    ppermute x1, starting transfers between devices: 2.64 us -> 5.47 us  [swap(): return lax.ppermute(array, 'core', [(0, 1), (1, 0)])]
  transfers between devices with their start and end apart: 6 -> 6, of which waited for: 1 -> 2; matrix products, arithmetic and copies ran while one was open for 0% -> 0% of each run, Pallas kernels for 3% -> 3%
where the time goes in v6:
time: 155 us; the launch traced here: 152 us
  blocking collectives  101 us (65%)
  starting transfers between devices  23.2 us (15%)
  Pallas kernels  17.6 us (11%)
  waiting for transfers between devices  9.89 us (6%)
    all_to_all x2, blocking collectives, exchange(): lax.all_to_all(array, ('col', 'replica'), split_axis=0, concat_axis=0, ti...  101 us
    ppermute x2, starting transfers between devices, local(): lax.ppermute(spread[step], line, factor_pairs(step))  12.8 us
    pallas_call x1, Pallas kernels, precondition(): pl.pallas_call(block_kernel, out_shape=jax.ShapeDtypeStruct((COLS * RING,...  6.08 us
    ppermute x1, starting transfers between devices, swap(): return lax.ppermute(array, 'core', [(0, 1), (1, 0)])  5.47 us
    ppermute x1, waiting for transfers between devices, swap(): return lax.ppermute(array, 'core', [(0, 1), (1, 0)])  5.26 us
    pallas_call x1, Pallas kernels, prepare(): pl.pallas_call(prepare_kernel, out_shape=[jax.ShapeDtypeStruct(second.sha...  5.08 us
    ppermute x2, waiting for transfers between devices, local(): lax.ppermute(shard, line, factor_pairs(EARLY + at))  4.62 us
    ppermute x2, starting transfers between devices, local(): lax.ppermute(shard, line, factor_pairs(EARLY + at))  4.25 us
  transfers between devices with their start and end apart: 6, of which 2 were waited for; matrix products, arithmetic and copies ran while one was open for 0% of the time, Pallas kernels for 3%

profile of v6, /device:TPU:1, one launch (start us, length us, event | category | flops | bytes accessed | tf_op | source)
XLA Modules:
  0.0 152.4 jit_solution(8449537669140242649)
XLA Ops:
  0.6 2.7 %spread_factors.1 = (bf16[16,128,128]{2,1,0:T(8,128)(2,1)}, bf16[16,128,128]{2,1,0:T(8,128)(2,1)}, bf16[16,128,128]{2,1,0:T(8,128)(2,1)}, bf16[16,128,128]{2,1,0:T(8,128)(2,1)}) custom-call(bf16[3,128,1024]{2,1,0:T(8,128)(2,1)} %left.1, bf16[3,1024,128]{2,1,0:T(8,128)(2,1)} %right.1), custom_call_target="tpu_custom_call" | custom-call | tf_op jit(solution)/shard_map/spread_factors/pallas_call | solution.py:102
  3.3 11.5 %collective-permute-start = (bf16[16,128,128]{2,1,0:T(8,128)(2,1)}, bf16[16,128,128]{2,1,0:T(8,128)(2,1)}, u32[]{:S(2)}, u32[]{:S(2)}) collective-permute-start(bf16[16,128,128]{2,1,0:T(8,128)(2,1)} %get-tuple-element.15.after.own), channel_id=1, source_target_pairs={{4,8},{5,0},{6,10},{8,13},{9,5},{10,6},{20,24},{21,16},{22,26},{24... | collective-permute-start | bytes 1572872 | tf_op jit(solution)/shard_map/ppermute | solution.py:390
  14.8 1.3 collective-permute-start.2
  16.1 5.1 %prepare.1 = (bf16[16,16,8,128]{3,2,1,0:T(8,128)(2,1)}, bf16[256,16,128]{2,1,0:T(8,128)(2,1)}, s32[2,128]{1,0:T(2,128)}) custom-call(s32[3,64]{1,0:T(4,128)} %bitcast.1, bf16[16,16,8,128]{3,2,1,0:T(8,128)(2,1)} %gradient.1, bf16[16,16,8,128]{3,2,1,0:T(8,128)(2,1)} %second.1, bf16[16,128,128]{2,1,0:T(8,128)(2,1)} %get-tuple-element.15.after.own), custom_call_target="tpu_custom_call" | custom-call | tf_op jit(solution)/shard_map/prepare/pallas_call | solution.py:178
  21.2 0.0 copy-start
  21.2 2.3 %collective-permute-start.3 = (bf16[16,128,128]{2,1,0:T(8,128)(2,1)}, bf16[16,128,128]{2,1,0:T(8,128)(2,1)}, u32[]{:S(2)}, u32[]{:S(2)}) collective-permute-start(bf16[16,128,128]{2,1,0:T(8,128)(2,1)} %get-tuple-element.21), channel_id=1, source_target_pairs={{2,0},{6,8},{3,1},{7,9},{4,2},{0,10},{14,12},{10,4},{15,13},{11,5}... | collective-permute-start | bytes 1572872 | tf_op jit(solution)/shard_map/ppermute | solution.py:393
  23.5 1.9 %collective-permute-start.4 = (bf16[16,128,128]{2,1,0:T(8,128)(2,1)}, bf16[16,128,128]{2,1,0:T(8,128)(2,1)}, u32[]{:S(2)}, u32[]{:S(2)}) collective-permute-start(bf16[16,128,128]{2,1,0:T(8,128)(2,1)} %get-tuple-element.22), channel_id=1, source_target_pairs={{3,0},{7,8},{4,1},{0,9},{5,2},{1,10},{15,12},{11,4},{8,13},{12,5},... | collective-permute-start | bytes 1572872 | tf_op jit(solution)/shard_map/ppermute | solution.py:393
  25.4 0.0 collective-permute-done.refs_0_
  25.5 0.7 collective-permute-start.1
  26.2 58.0 %conditional.1 = (bf16[256,16,128]{2,1,0:T(8,128)(2,1)S(1)}) conditional(s32[]{:T(128)} %convert_element_type.3, () %tuple.14, bf16[256,16,128]{2,1,0:T(8,128)(2,1)} %get-tuple-element.17.refs_1_.refs_2_), branch_computations={%region_0.0_spmd, %region_1.0_spmd} | conditional | bytes 2097160 | solution.py:396
  26.2 58.0 %all_to_all.9 = bf16[256,16,128]{2,1,0:T(8,128)(2,1)S(1)} all-to-all(bf16[256,16,128]{2,1,0:T(8,128)(2,1)} %param.1), channel_id=1, replica_groups=mesh['col'=32,'core'=2,'replica'=8] {'col','replica'}, dimensions={0} | all-to-all | bytes 2097152 | tf_op jit(solution)/shard_map/cond/branch_1_fun/all_to_all | solution.py:380
  84.2 0.0 collective-permute-done.2.refs_1_
  84.2 0.0 collective-permute-done.3.refs_2_
  84.2 4.6 %collective-permute-done.4.refs_3_ = bf16[16,128,128]{2,1,0:T(8,128)(2,1)} collective-permute-done((bf16[16,128,128]{2,1,0:T(8,128)(2,1)}, bf16[16,128,128]{2,1,0:T(8,128)(2,1)}, u32[]{:S(2)}, u32[]{:S(2)}) %collective-permute-start.4) | collective-permute-done | bytes 524320 | tf_op jit(solution)/shard_map/ppermute | solution.py:393
  88.8 0.0 collective-permute-done.1.relayed
  88.8 0.0 copy-done
  88.8 1.7 %together.1.own = bf16[768,16,128]{2,1,0:T(8,128)(2,1)S(1)} custom-call(bf16[256,16,128]{2,1,0:T(8,128)(2,1)S(1)} %get-tuple-element.24.columns, bf16[16,128,128]{2,1,0:T(8,128)(2,1)S(1)} %copy-done, bf16[16,128,128]{2,1,0:T(8,128)(2,1)S(1)} %collective-permute-done.1.relayed, bf16[16,128,128]{2,1,0:T(8,128)(2,1)} %released.2.refs_0_, ...), custom_call_target="tpu_custom_call" | custom-call | tf_op jit(solution)/shard_map/together/pallas_call | solution.py:246
  90.5 0.0 copy-start.1
  90.5 0.0 copy-start.2
  90.6 5.5 %collective-permute-start.5 = (bf16[768,16,128]{2,1,0:T(8,128)(2,1)S(1)}, bf16[768,16,128]{2,1,0:T(8,128)(2,1)S(1)}, u32[]{:S(2)}, u32[]{:S(2)}) collective-permute-start(bf16[768,16,128]{2,1,0:T(8,128)(2,1)S(1)} %together.1.own), channel_id=1, source_target_pairs={{0,8},{8,0},{1,9},{9,1},{2,10},{10,2},{3,11},{11,3},{4,12},{12,4},... | collective-permute-start | bytes 9437192 | tf_op jit(solution)/shard_map/ppermute | solution.py:384
  96.0 5.3 %collective-permute-done.5.swapped = bf16[768,16,128]{2,1,0:T(8,128)(2,1)S(1)} collective-permute-done((bf16[768,16,128]{2,1,0:T(8,128)(2,1)S(1)}, bf16[768,16,128]{2,1,0:T(8,128)(2,1)S(1)}, u32[]{:S(2)}, u32[]{:S(2)}) %collective-permute-start.5) | collective-permute-done | bytes 3145760 | tf_op jit(solution)/shard_map/ppermute | solution.py:384
  101.3 6.1 %precondition.1 = bf16[256,16,128]{2,1,0:T(8,128)(2,1)S(1)} custom-call(bf16[768,16,128]{2,1,0:T(8,128)(2,1)S(1)} %together.1.own, bf16[768,16,128]{2,1,0:T(8,128)(2,1)S(1)} %collective-permute-done.5.swapped), custom_call_target="tpu_custom_call" | custom-call | flops 4294967296 | bytes 10485760 | tf_op jit(solution)/shard_map/precondition/pallas_call | solution.py:324
  107.4 43.0 %all_to_all.10.returned = bf16[256,16,128]{2,1,0:T(8,128)(2,1)S(1)} all-to-all(bf16[256,16,128]{2,1,0:T(8,128)(2,1)S(1)} %precondition.1), channel_id=1, replica_groups=mesh['col'=32,'core'=2,'replica'=8] {'col','replica'}, dimensions={0} | all-to-all | bytes 2097152 | tf_op jit(solution)/shard_map/all_to_all | solution.py:380
  150.4 0.0 copy-done.1
  150.4 0.0 copy-done.2
  150.4 2.1 %finish.1 = bf16[16,16,8,128]{3,2,1,0:T(8,128)(2,1)} custom-call(s32[2,128]{1,0:T(2,128)S(1)} %copy-done.2, bf16[256,16,128]{2,1,0:T(8,128)(2,1)S(1)} %all_to_all.10.returned, bf16[16,16,8,128]{3,2,1,0:T(8,128)(2,1)S(1)} %copy-done.1), custom_call_target="tpu_custom_call" | custom-call | tf_op jit(solution)/shard_map/finish/pallas_call | solution.py:365
  (2 shorter events, 0.0 us)
Async XLA Ops:
  3.3 22.2 %collective-permute-start = (bf16[16,128,128]{2,1,0:T(8,128)(2,1)}, bf16[16,128,128]{2,1,0:T(8,128)(2,1)}, u32[]{:S(2)}, u32[]{:S(2)}) collective-permute-start(bf16[16,128,128]{2,1,0:T(8,128)(2,1)} %get-tuple-element.15.after.own), channel_id=1, source_target_pairs={{4,8},{5,0},{6,10},{8,13},{9,5},{10,6},{20,24},{21,16},{22,26},{24... | collective-permute-start | bytes 1572872 | tf_op jit(solution)/shard_map/ppermute | solution.py:390
  14.8 69.4 %collective-permute-start.2 = (bf16[16,128,128]{2,1,0:T(8,128)(2,1)}, bf16[16,128,128]{2,1,0:T(8,128)(2,1)}, u32[]{:S(2)}, u32[]{:S(2)}) collective-permute-start(bf16[16,128,128]{2,1,0:T(8,128)(2,1)} %get-tuple-element.18), channel_id=1, source_target_pairs={{1,0},{5,8},{2,1},{6,9},{3,2},{7,10},{13,12},{9,4},{14,13},{10,5},... | collective-permute-start | bytes 1572872 | tf_op jit(solution)/shard_map/ppermute | solution.py:390
  21.2 67.6 %copy-start = (bf16[16,128,128]{2,1,0:T(8,128)(2,1)S(1)}, bf16[16,128,128]{2,1,0:T(8,128)(2,1)}, u32[]{:S(2)}) copy-start(bf16[16,128,128]{2,1,0:T(8,128)(2,1)} %get-tuple-element.15.after.own) | copy-start | bytes 1572868
  21.2 63.0 %collective-permute-start.3 = (bf16[16,128,128]{2,1,0:T(8,128)(2,1)}, bf16[16,128,128]{2,1,0:T(8,128)(2,1)}, u32[]{:S(2)}, u32[]{:S(2)}) collective-permute-start(bf16[16,128,128]{2,1,0:T(8,128)(2,1)} %get-tuple-element.21), channel_id=1, source_target_pairs={{2,0},{6,8},{3,1},{7,9},{4,2},{0,10},{14,12},{10,4},{15,13},{11,5}... | collective-permute-start | bytes 1572872 | tf_op jit(solution)/shard_map/ppermute | solution.py:393
  23.5 65.3 %collective-permute-start.4 = (bf16[16,128,128]{2,1,0:T(8,128)(2,1)}, bf16[16,128,128]{2,1,0:T(8,128)(2,1)}, u32[]{:S(2)}, u32[]{:S(2)}) collective-permute-start(bf16[16,128,128]{2,1,0:T(8,128)(2,1)} %get-tuple-element.22), channel_id=1, source_target_pairs={{3,0},{7,8},{4,1},{0,9},{5,2},{1,10},{15,12},{11,4},{8,13},{12,5},... | collective-permute-start | bytes 1572872 | tf_op jit(solution)/shard_map/ppermute | solution.py:393
  25.5 63.3 %collective-permute-start.1 = (bf16[16,128,128]{2,1,0:T(8,128)(2,1)}, bf16[16,128,128]{2,1,0:T(8,128)(2,1)S(1)}, u32[]{:S(2)}, u32[]{:S(2)}) collective-permute-start(bf16[16,128,128]{2,1,0:T(8,128)(2,1)} %released.2.refs_0_), channel_id=1, source_target_pairs={{0,9},{13,4},{16,25},{29,20},{32,41},{45,36},{48,57},{61,52},{64,7... | collective-permute-start | bytes 1572872 | tf_op jit(solution)/shard_map/ppermute | solution.py:395
  90.5 59.8 %copy-start.1 = (bf16[16,16,8,128]{3,2,1,0:T(8,128)(2,1)S(1)}, bf16[16,16,8,128]{3,2,1,0:T(8,128)(2,1)}, u32[]{:S(2)}) copy-start(bf16[16,16,8,128]{3,2,1,0:T(8,128)(2,1)} %momentum.1) | copy-start | bytes 1572868
  90.5 59.8 %copy-start.2 = (s32[2,128]{1,0:T(2,128)S(1)}, s32[2,128]{1,0:T(2,128)}, u32[]{:S(2)}) copy-start(s32[2,128]{1,0:T(2,128)} %get-tuple-element.16.place) | copy-start | bytes 3076
  90.6 10.7 %collective-permute-start.5 = (bf16[768,16,128]{2,1,0:T(8,128)(2,1)S(1)}, bf16[768,16,128]{2,1,0:T(8,128)(2,1)S(1)}, u32[]{:S(2)}, u32[]{:S(2)}) collective-permute-start(bf16[768,16,128]{2,1,0:T(8,128)(2,1)S(1)} %together.1.own), channel_id=1, source_target_pairs={{0,8},{8,0},{1,9},{9,1},{2,10},{10,2},{3,11},{11,3},{4,12},{12,4},... | collective-permute-start | bytes 9437192 | tf_op jit(solution)/shard_map/ppermute | solution.py:384

commit v7 on v6

--- a/solution.py
+++ b/solution.py
@@ -18,8 +18,7 @@
 CORES = 2
 NOTE = 3
 CHUNKS = 4
-RELAYED = (1, 0)
-BESIDE = (-1, 1)
+TURN = 2
 EARLY = 2
 
 ANY = pl.BlockSpec(memory_space=pl.ANY)
@@ -41,34 +40,30 @@
     return col * RING + place
 
 
+def chip_of(place):
+    return (place + TURN) % RING
+
+
+def place_here():
+    return lax.rem(lax.axis_index("replica") + RING - TURN, RING)
+
+
 def factor_pairs(step):
     pairs = []
     for c in range(CORES):
         for s in range(SLOTS):
-            root = PLACES * c + s
+            root = chip_of(PLACES * c + s)
             near, far = (root + step) % RING, (root + step + PLACES) % RING
             if step > 0:
                 pairs.append((c * RING + near, c * RING + root))
-                pairs.append((c * RING + far, (1 - c) * RING + root))
-            elif s == RELAYED[c]:
-                pairs.append((c * RING + far, c * RING + (root + BESIDE[c]) % RING))
-            else:
-                pairs.append((c * RING + far, (1 - c) * RING + root))
-    return pairs
-
-
-def relay_pairs():
-    pairs = []
-    for c in range(CORES):
-        root = PLACES * c + RELAYED[c]
-        pairs.append((c * RING + (root + BESIDE[c]) % RING, (1 - c) * RING + root))
+            pairs.append((c * RING + far, (1 - c) * RING + root))
     return pairs
 
 
 def factor_kernel(left, right, *refs):
     outs, held_left, held_right, spread, sems = refs[:PLACES], *refs[PLACES:]
     part = left.shape[1]
-    here = lax.axis_index("replica")
+    here = place_here()
     copies = []
     for s in range(SLOTS):
         copies.append(pltpu.make_async_copy(left.at[s], held_left.at[s], sems.at[0, s]))
@@ -153,7 +148,7 @@
                 i = lax.div(block, block_cols)
                 j = lax.rem(block, block_cols)
                 piece = wide[pl.ds(i * per_row + j, shard_rows, stride=block_cols), :]
-                pieces[member(col, PLACES * c + s)] = piece.astype(pieces.dtype)
+                pieces[member(col, chip_of(PLACES * c + s))] = piece.astype(pieces.dtype)
                 high, low = high_low(square[pl.ds(block, 1), :])
                 row = 2 * (SLOTS * c + s)
                 notes[row : row + 1, :] = high
@@ -161,10 +156,10 @@
 
                 @pl.when(held >= 0)
                 def _():
-                    place[0, block] = member(col, PLACES * c + s)
+                    place[0, block] = member(col, chip_of(PLACES * c + s))
                     place[1, block] = col * shard_rows + row
 
-        pieces[member(col, NOTE)] = notes[...].astype(pieces.dtype)
+        pieces[member(col, chip_of(NOTE))] = notes[...].astype(pieces.dtype)
         return carry
 
     lax.fori_loop(0, COLS, column, 0)
@@ -215,14 +210,11 @@
     )(*arrays, other)
 
 
-def together_kernel(columns, own, relayed, *refs):
+def together_kernel(columns, own, *refs):
     factors, out = refs[:PLACES], refs[PLACES]
     count, rows, part = columns.shape
     size = own.shape[0] * own.shape[1] // rows
-    here = lax.axis_index("replica")
-    at_home = lax.div(here, PLACES) == lax.axis_index("core")
-    slot = lax.rem(here, PLACES)
-    direct = slot != jnp.where(here < PLACES, RELAYED[0], RELAYED[1])
+    at_home = lax.div(place_here(), PLACES) == lax.axis_index("core")
     out[:count] = columns[...]
     for step in range(1, PLACES):
         out[count + step * size : count + (step + 1) * size] = factors[step][...].reshape(size, rows, part)
@@ -231,13 +223,9 @@
     def _():
         out[count : count + size] = own[...].reshape(size, rows, part)
 
-    @pl.when(jnp.logical_not(at_home) & direct)
+    @pl.when(jnp.logical_not(at_home))
     def _():
         out[count : count + size] = factors[0][...].reshape(size, rows, part)
-
-    @pl.when(jnp.logical_not(at_home) & jnp.logical_not(direct))
-    def _():
-        out[count : count + size] = relayed[...].reshape(size, rows, part)
 
 
 def together(columns, shards):
@@ -260,11 +248,11 @@
     groups = part // rows
     core = lax.axis_index("core")
     here = lax.axis_index("replica")
-    place = lax.rem(here, PLACES)
+    place = lax.rem(place_here(), PLACES)
 
     @pl.when(place < SLOTS)
     def _():
-        owner_core = lax.div(here, PLACES)
+        owner_core = lax.div(place_here(), PLACES)
         for b, held in enumerate((own, swapped)):
             h = core if b == 0 else 1 - core
             for col in range(COLS):
@@ -343,7 +331,7 @@
 def finish_kernel(place, returned, momentum, out, wide, adam):
     block_rows, shard_rows, block_cols, lanes = momentum.shape
     for col in range(COLS):
-        note = jnp.sum(returned[member(col, NOTE)].astype(jnp.float32), axis=1, keepdims=True)
+        note = jnp.sum(returned[member(col, chip_of(NOTE))].astype(jnp.float32), axis=1, keepdims=True)
         adam[col * shard_rows : (col + 1) * shard_rows, :] = jnp.broadcast_to(note, (shard_rows, lanes))
 
     def step(i, carry):
@@ -391,10 +379,8 @@
     moment_new, pieces, place = prepare(block_of_slot.T, gradient, second_moment, spread[0])
     later = released(spread[EARLY:], pieces)
     factors += [lax.ppermute(shard, line, factor_pairs(EARLY + at)) for at, shard in enumerate(later)]
-    factors[:1] = released(factors[:1], pieces)
-    relayed = lax.ppermute(factors[0], line, relay_pairs())
     columns = lax.cond(lax.axis_index("core") < CORES, exchange, jnp.zeros_like, pieces)
-    held = together(columns, [spread[0], relayed] + factors)
+    held = together(columns, [spread[0]] + factors)
     parts = precondition(held, swap(held))
     return (finish(place, exchange(parts), momentum), moment_new)
 

time: 155 us -> 150 us (0.968)
  starting transfers between devices: 23.2 us -> 18.3 us
  waiting for transfers between devices: 9.89 us -> 5.64 us
  blocking collectives: 101 us -> 105 us
    ppermute x2, waiting for transfers between devices: 4.62 us -> 0.01 us  [local(): lax.ppermute(shard, line, factor_pairs(EARLY + at))]
    all_to_all x2, blocking collectives: 101 us -> 105 us  [exchange(): lax.all_to_all(array, ('col', 'replica'), split_axis=0, concat_axis=0, ti...]
    ppermute x1, starting transfers between devices: 5.47 us -> 2.05 us  [swap(): return lax.ppermute(array, 'core', [(0, 1), (1, 0)])]
  transfers between devices with their start and end apart: 6 -> 5, of which waited for: 2 -> 1; matrix products, arithmetic and copies ran while one was open for 0% -> 0% of each run, Pallas kernels for 3% -> 4%
where the time goes in v7:
time: 150 us; the launch traced here: 147 us
  blocking collectives  105 us (70%)
  starting transfers between devices  18.3 us (12%)
  Pallas kernels  17.6 us (12%)
  waiting for transfers between devices  5.64 us (4%)
    all_to_all x2, blocking collectives, exchange(): lax.all_to_all(array, ('col', 'replica'), split_axis=0, concat_axis=0, ti...  105 us
    ppermute x2, starting transfers between devices, local(): lax.ppermute(spread[step], line, factor_pairs(step))  13 us
    pallas_call x1, Pallas kernels, precondition(): pl.pallas_call(block_kernel, out_shape=jax.ShapeDtypeStruct((COLS * RING,...  6.14 us
    ppermute x1, waiting for transfers between devices, swap(): return lax.ppermute(array, 'core', [(0, 1), (1, 0)])  5.63 us
    pallas_call x1, Pallas kernels, prepare(): pl.pallas_call(prepare_kernel, out_shape=[jax.ShapeDtypeStruct(second.sha...  5.28 us
    ppermute x2, starting transfers between devices, local(): lax.ppermute(shard, line, factor_pairs(EARLY + at))  3.21 us
  transfers between devices with their start and end apart: 5, of which 1 were waited for; matrix products, arithmetic and copies ran while one was open for 0% of the time, Pallas kernels for 4%

profile of v7, /device:TPU:1, one launch (start us, length us, event | category | flops | bytes accessed | tf_op | source)
XLA Modules:
  0.0 147.4 jit_solution(1833016317259649464)
XLA Ops:
  0.6 2.7 %spread_factors.1 = (bf16[16,128,128]{2,1,0:T(8,128)(2,1)}, bf16[16,128,128]{2,1,0:T(8,128)(2,1)}, bf16[16,128,128]{2,1,0:T(8,128)(2,1)}, bf16[16,128,128]{2,1,0:T(8,128)(2,1)}) custom-call(bf16[3,128,1024]{2,1,0:T(8,128)(2,1)} %left.1, bf16[3,1024,128]{2,1,0:T(8,128)(2,1)} %right.1), custom_call_target="tpu_custom_call" | custom-call | tf_op jit(solution)/shard_map/spread_factors/pallas_call | solution.py:97
  3.3 11.5 %collective-permute-start.1 = (bf16[16,128,128]{2,1,0:T(8,128)(2,1)}, bf16[16,128,128]{2,1,0:T(8,128)(2,1)}, u32[]{:S(2)}, u32[]{:S(2)}) collective-permute-start(bf16[16,128,128]{2,1,0:T(8,128)(2,1)} %get-tuple-element.18), channel_id=1, source_target_pairs={{3,2},{7,10},{4,3},{0,11},{5,4},{1,12},{15,14},{11,6},{8,15},{12,7... | collective-permute-start | bytes 1572872 | tf_op jit(solution)/shard_map/ppermute | solution.py:378
  14.8 1.5 %collective-permute-start = (bf16[16,128,128]{2,1,0:T(8,128)(2,1)}, bf16[16,128,128]{2,1,0:T(8,128)(2,1)}, u32[]{:S(2)}, u32[]{:S(2)}) collective-permute-start(bf16[16,128,128]{2,1,0:T(8,128)(2,1)} %get-tuple-element.15.after.own), channel_id=1, source_target_pairs={{6,10},{7,11},{0,12},{10,6},{11,7},{12,0},{22,26},{23,27},{16,28},... | collective-permute-start | bytes 1572872 | tf_op jit(solution)/shard_map/ppermute | solution.py:378
  16.3 0.0 copy-start
  16.3 5.3 %prepare.1 = (bf16[16,16,8,128]{3,2,1,0:T(8,128)(2,1)}, bf16[256,16,128]{2,1,0:T(8,128)(2,1)}, s32[2,128]{1,0:T(2,128)}) custom-call(s32[3,64]{1,0:T(4,128)} %bitcast.1, bf16[16,16,8,128]{3,2,1,0:T(8,128)(2,1)} %gradient.1, bf16[16,16,8,128]{3,2,1,0:T(8,128)(2,1)} %second.1, bf16[16,128,128]{2,1,0:T(8,128)(2,1)} %get-tuple-element.15.after.own), custom_call_target="tpu_custom_call" | custom-call | tf_op jit(solution)/shard_map/prepare/pallas_call | solution.py:173
  21.6 1.9 %collective-permute-start.2 = (bf16[16,128,128]{2,1,0:T(8,128)(2,1)}, bf16[16,128,128]{2,1,0:T(8,128)(2,1)S(1)}, u32[]{:S(2)}, u32[]{:S(2)}) collective-permute-start(bf16[16,128,128]{2,1,0:T(8,128)(2,1)} %get-tuple-element.21), channel_id=1, source_target_pairs={{4,2},{0,10},{5,3},{1,11},{6,4},{2,12},{8,14},{12,6},{9,15},{13,7}... | collective-permute-start | bytes 1572872 | tf_op jit(solution)/shard_map/ppermute | solution.py:381
  23.5 1.3 collective-permute-start.3
  24.8 60.4 %conditional.1 = (bf16[256,16,128]{2,1,0:T(8,128)(2,1)S(1)}) conditional(s32[]{:T(128)} %convert_element_type.3, () %tuple.14, bf16[256,16,128]{2,1,0:T(8,128)(2,1)} %get-tuple-element.17.refs_2_), branch_computations={%region_0.0_spmd, %region_1.0_spmd} | conditional | bytes 2097160 | solution.py:382
  24.8 60.4 %all_to_all.9 = bf16[256,16,128]{2,1,0:T(8,128)(2,1)S(1)} all-to-all(bf16[256,16,128]{2,1,0:T(8,128)(2,1)} %param.1), channel_id=1, replica_groups=mesh['col'=32,'core'=2,'replica'=8] {'col','replica'}, dimensions={0} | all-to-all | bytes 2097152 | tf_op jit(solution)/shard_map/cond/branch_1_fun/all_to_all | solution.py:368
  85.2 0.0 collective-permute-done.1.refs_1_
  85.2 0.0 collective-permute-done.refs_0_
  85.2 0.0 collective-permute-done.2.refs_2_
  85.2 0.0 collective-permute-done.3.refs_3_
  85.2 0.0 copy-done
  85.3 1.4 together.1.own
  86.7 0.0 copy-start.1
  86.7 0.0 copy-start.2
  86.7 2.1 %collective-permute-start.4 = (bf16[768,16,128]{2,1,0:T(8,128)(2,1)S(1)}, bf16[768,16,128]{2,1,0:T(8,128)(2,1)S(1)}, u32[]{:S(2)}, u32[]{:S(2)}) collective-permute-start(bf16[768,16,128]{2,1,0:T(8,128)(2,1)S(1)} %together.1.own), channel_id=1, source_target_pairs={{0,8},{8,0},{1,9},{9,1},{2,10},{10,2},{3,11},{11,3},{4,12},{12,4},... | collective-permute-start | bytes 9437192 | tf_op jit(solution)/shard_map/ppermute | solution.py:372
  88.8 5.6 %collective-permute-done.4.swapped = bf16[768,16,128]{2,1,0:T(8,128)(2,1)S(1)} collective-permute-done((bf16[768,16,128]{2,1,0:T(8,128)(2,1)S(1)}, bf16[768,16,128]{2,1,0:T(8,128)(2,1)S(1)}, u32[]{:S(2)}, u32[]{:S(2)}) %collective-permute-start.4) | collective-permute-done | bytes 3145760 | tf_op jit(solution)/shard_map/ppermute | solution.py:372
  94.4 6.1 %precondition.1 = bf16[256,16,128]{2,1,0:T(8,128)(2,1)S(1)} custom-call(bf16[768,16,128]{2,1,0:T(8,128)(2,1)S(1)} %together.1.own, bf16[768,16,128]{2,1,0:T(8,128)(2,1)S(1)} %collective-permute-done.4.swapped), custom_call_target="tpu_custom_call" | custom-call | flops 4294967296 | bytes 10485760 | tf_op jit(solution)/shard_map/precondition/pallas_call | solution.py:312
  100.5 44.8 %all_to_all.10.returned = bf16[256,16,128]{2,1,0:T(8,128)(2,1)S(1)} all-to-all(bf16[256,16,128]{2,1,0:T(8,128)(2,1)S(1)} %precondition.1), channel_id=1, replica_groups=mesh['col'=32,'core'=2,'replica'=8] {'col','replica'}, dimensions={0} | all-to-all | bytes 2097152 | tf_op jit(solution)/shard_map/all_to_all | solution.py:368
  145.3 0.0 copy-done.1
  145.3 0.0 copy-done.2
  145.3 2.1 %finish.1 = bf16[16,16,8,128]{3,2,1,0:T(8,128)(2,1)} custom-call(s32[2,128]{1,0:T(2,128)S(1)} %copy-done.2, bf16[256,16,128]{2,1,0:T(8,128)(2,1)S(1)} %all_to_all.10.returned, bf16[16,16,8,128]{3,2,1,0:T(8,128)(2,1)S(1)} %copy-done.1), custom_call_target="tpu_custom_call" | custom-call | tf_op jit(solution)/shard_map/finish/pallas_call | solution.py:353
  (1 shorter events, 0.0 us)
Async XLA Ops:
  3.3 81.9 %collective-permute-start.1 = (bf16[16,128,128]{2,1,0:T(8,128)(2,1)}, bf16[16,128,128]{2,1,0:T(8,128)(2,1)}, u32[]{:S(2)}, u32[]{:S(2)}) collective-permute-start(bf16[16,128,128]{2,1,0:T(8,128)(2,1)} %get-tuple-element.18), channel_id=1, source_target_pairs={{3,2},{7,10},{4,3},{0,11},{5,4},{1,12},{15,14},{11,6},{8,15},{12,7... | collective-permute-start | bytes 1572872 | tf_op jit(solution)/shard_map/ppermute | solution.py:378
  14.8 70.4 %collective-permute-start = (bf16[16,128,128]{2,1,0:T(8,128)(2,1)}, bf16[16,128,128]{2,1,0:T(8,128)(2,1)}, u32[]{:S(2)}, u32[]{:S(2)}) collective-permute-start(bf16[16,128,128]{2,1,0:T(8,128)(2,1)} %get-tuple-element.15.after.own), channel_id=1, source_target_pairs={{6,10},{7,11},{0,12},{10,6},{11,7},{12,0},{22,26},{23,27},{16,28},... | collective-permute-start | bytes 1572872 | tf_op jit(solution)/shard_map/ppermute | solution.py:378
  16.3 68.9 %copy-start = (bf16[16,128,128]{2,1,0:T(8,128)(2,1)S(1)}, bf16[16,128,128]{2,1,0:T(8,128)(2,1)}, u32[]{:S(2)}) copy-start(bf16[16,128,128]{2,1,0:T(8,128)(2,1)} %get-tuple-element.15.after.own) | copy-start | bytes 1572868
  21.6 63.6 %collective-permute-start.2 = (bf16[16,128,128]{2,1,0:T(8,128)(2,1)}, bf16[16,128,128]{2,1,0:T(8,128)(2,1)S(1)}, u32[]{:S(2)}, u32[]{:S(2)}) collective-permute-start(bf16[16,128,128]{2,1,0:T(8,128)(2,1)} %get-tuple-element.21), channel_id=1, source_target_pairs={{4,2},{0,10},{5,3},{1,11},{6,4},{2,12},{8,14},{12,6},{9,15},{13,7}... | collective-permute-start | bytes 1572872 | tf_op jit(solution)/shard_map/ppermute | solution.py:381
  23.5 61.7 %collective-permute-start.3 = (bf16[16,128,128]{2,1,0:T(8,128)(2,1)}, bf16[16,128,128]{2,1,0:T(8,128)(2,1)S(1)}, u32[]{:S(2)}, u32[]{:S(2)}) collective-permute-start(bf16[16,128,128]{2,1,0:T(8,128)(2,1)} %get-tuple-element.22), channel_id=1, source_target_pairs={{5,2},{1,10},{6,3},{2,11},{7,4},{3,12},{9,14},{13,6},{10,15},{14,7... | collective-permute-start | bytes 1572872 | tf_op jit(solution)/shard_map/ppermute | solution.py:381
  86.7 58.6 %copy-start.1 = (bf16[16,16,8,128]{3,2,1,0:T(8,128)(2,1)S(1)}, bf16[16,16,8,128]{3,2,1,0:T(8,128)(2,1)}, u32[]{:S(2)}) copy-start(bf16[16,16,8,128]{3,2,1,0:T(8,128)(2,1)} %momentum.1) | copy-start | bytes 1572868
  86.7 58.6 %copy-start.2 = (s32[2,128]{1,0:T(2,128)S(1)}, s32[2,128]{1,0:T(2,128)}, u32[]{:S(2)}) copy-start(s32[2,128]{1,0:T(2,128)} %get-tuple-element.16.place) | copy-start | bytes 3076
  86.7 7.7 %collective-permute-start.4 = (bf16[768,16,128]{2,1,0:T(8,128)(2,1)S(1)}, bf16[768,16,128]{2,1,0:T(8,128)(2,1)S(1)}, u32[]{:S(2)}, u32[]{:S(2)}) collective-permute-start(bf16[768,16,128]{2,1,0:T(8,128)(2,1)S(1)} %together.1.own), channel_id=1, source_target_pairs={{0,8},{8,0},{1,9},{9,1},{2,10},{10,2},{3,11},{11,3},{4,12},{12,4},... | collective-permute-start | bytes 9437192 | tf_op jit(solution)/shard_map/ppermute | solution.py:372

commit v8 on v7

--- a/solution.py
+++ b/solution.py
@@ -19,7 +19,7 @@
 NOTE = 3
 CHUNKS = 4
 TURN = 2
-EARLY = 2
+EARLY = 3
 
 ANY = pl.BlockSpec(memory_space=pl.ANY)
 HBM = pl.BlockSpec(memory_space=pltpu.HBM)

time: 150 us -> 150 us (level)
    ppermute x2 -> x1, starting transfers between devices: 3.21 us -> 1.29 us  [local(): lax.ppermute(shard, line, factor_pairs(EARLY + at))]
    ppermute x2 -> x3, starting transfers between devices: 13 us -> 14.9 us  [local(): lax.ppermute(spread[step], line, factor_pairs(step))]
where the time goes in v8:
time: 150 us; the launch traced here: 148 us
  blocking collectives  105 us (70%)
  starting transfers between devices  18.2 us (12%)
  Pallas kernels  17.7 us (12%)
  waiting for transfers between devices  5.64 us (4%)
    all_to_all x2, blocking collectives, exchange(): lax.all_to_all(array, ('col', 'replica'), split_axis=0, concat_axis=0, ti...  105 us
    ppermute x3, starting transfers between devices, local(): lax.ppermute(spread[step], line, factor_pairs(step))  14.9 us
    pallas_call x1, Pallas kernels, precondition(): pl.pallas_call(block_kernel, out_shape=jax.ShapeDtypeStruct((COLS * RING,...  6.14 us
    ppermute x1, waiting for transfers between devices, swap(): return lax.ppermute(array, 'core', [(0, 1), (1, 0)])  5.63 us
    pallas_call x1, Pallas kernels, prepare(): pl.pallas_call(prepare_kernel, out_shape=[jax.ShapeDtypeStruct(second.sha...  5.29 us
  transfers between devices with their start and end apart: 5, of which 1 were waited for; matrix products, arithmetic and copies ran while one was open for 0% of the time, Pallas kernels for 4%

profile of v8, /device:TPU:1, one launch (start us, length us, event | category | flops | bytes accessed | tf_op | source)
XLA Modules:
  0.0 147.6 jit_solution(844604118374020112)
XLA Ops:
  0.6 2.7 %spread_factors.1 = (bf16[16,128,128]{2,1,0:T(8,128)(2,1)}, bf16[16,128,128]{2,1,0:T(8,128)(2,1)}, bf16[16,128,128]{2,1,0:T(8,128)(2,1)}, bf16[16,128,128]{2,1,0:T(8,128)(2,1)}) custom-call(bf16[3,128,1024]{2,1,0:T(8,128)(2,1)} %left.1, bf16[3,1024,128]{2,1,0:T(8,128)(2,1)} %right.1), custom_call_target="tpu_custom_call" | custom-call | tf_op jit(solution)/shard_map/spread_factors/pallas_call | solution.py:97
  3.3 11.5 %collective-permute-start.1 = (bf16[16,128,128]{2,1,0:T(8,128)(2,1)}, bf16[16,128,128]{2,1,0:T(8,128)(2,1)}, u32[]{:S(2)}, u32[]{:S(2)}) collective-permute-start(bf16[16,128,128]{2,1,0:T(8,128)(2,1)} %get-tuple-element.16), channel_id=1, source_target_pairs={{3,2},{7,10},{4,3},{0,11},{5,4},{1,12},{15,14},{11,6},{8,15},{12,7... | collective-permute-start | bytes 1572872 | tf_op jit(solution)/shard_map/ppermute | solution.py:378
  14.8 1.9 %collective-permute-start.2 = (bf16[16,128,128]{2,1,0:T(8,128)(2,1)}, bf16[16,128,128]{2,1,0:T(8,128)(2,1)}, u32[]{:S(2)}, u32[]{:S(2)}) collective-permute-start(bf16[16,128,128]{2,1,0:T(8,128)(2,1)} %get-tuple-element.17), channel_id=1, source_target_pairs={{4,2},{0,10},{5,3},{1,11},{6,4},{2,12},{8,14},{12,6},{9,15},{13,7}... | collective-permute-start | bytes 1572872 | tf_op jit(solution)/shard_map/ppermute | solution.py:378
  16.7 1.5 %collective-permute-start = (bf16[16,128,128]{2,1,0:T(8,128)(2,1)}, bf16[16,128,128]{2,1,0:T(8,128)(2,1)}, u32[]{:S(2)}, u32[]{:S(2)}) collective-permute-start(bf16[16,128,128]{2,1,0:T(8,128)(2,1)} %get-tuple-element.13.after.own), channel_id=1, source_target_pairs={{6,10},{7,11},{0,12},{10,6},{11,7},{12,0},{22,26},{23,27},{16,28},... | collective-permute-start | bytes 1572872 | tf_op jit(solution)/shard_map/ppermute | solution.py:378
  18.2 0.0 copy-start
  18.2 5.3 %prepare.1 = (bf16[16,16,8,128]{3,2,1,0:T(8,128)(2,1)}, bf16[256,16,128]{2,1,0:T(8,128)(2,1)}, s32[2,128]{1,0:T(2,128)}) custom-call(s32[3,64]{1,0:T(4,128)} %bitcast.1, bf16[16,16,8,128]{3,2,1,0:T(8,128)(2,1)} %gradient.1, bf16[16,16,8,128]{3,2,1,0:T(8,128)(2,1)} %second.1, bf16[16,128,128]{2,1,0:T(8,128)(2,1)} %get-tuple-element.13.after.own), custom_call_target="tpu_custom_call" | custom-call | tf_op jit(solution)/shard_map/prepare/pallas_call | solution.py:173
  23.5 1.3 collective-permute-start.3
  24.8 60.3 %conditional.1 = (bf16[256,16,128]{2,1,0:T(8,128)(2,1)S(1)}) conditional(s32[]{:T(128)} %convert_element_type.3, () %tuple.14, bf16[256,16,128]{2,1,0:T(8,128)(2,1)} %get-tuple-element.15.refs_1_), branch_computations={%region_0.0_spmd, %region_1.0_spmd} | conditional | bytes 2097160 | solution.py:382
  24.8 60.3 %all_to_all.9 = bf16[256,16,128]{2,1,0:T(8,128)(2,1)S(1)} all-to-all(bf16[256,16,128]{2,1,0:T(8,128)(2,1)} %param.1), channel_id=1, replica_groups=mesh['col'=32,'core'=2,'replica'=8] {'col','replica'}, dimensions={0} | all-to-all | bytes 2097152 | tf_op jit(solution)/shard_map/cond/branch_1_fun/all_to_all | solution.py:368
  85.2 0.0 collective-permute-done.1.refs_1_
  85.2 0.0 collective-permute-done.2.refs_2_
  85.2 0.0 collective-permute-done.refs_0_
  85.2 0.0 collective-permute-done.3.refs_3_
  85.2 0.0 copy-done
  85.2 1.6 %together.1.own = bf16[768,16,128]{2,1,0:T(8,128)(2,1)S(1)} custom-call(bf16[256,16,128]{2,1,0:T(8,128)(2,1)S(1)} %get-tuple-element.20.columns, bf16[16,128,128]{2,1,0:T(8,128)(2,1)S(1)} %copy-done, bf16[16,128,128]{2,1,0:T(8,128)(2,1)} %collective-permute-done.refs_0_, bf16[16,128,128]{2,1,0:T(8,128)(2,1)} %collective-permute-done.1.refs_1_, ...), custom_call_target="tpu_custom_call" | custom-call | tf_op jit(solution)/shard_map/together/pallas_call | solution.py:234
  86.8 0.0 copy-start.1
  86.8 0.0 copy-start.2
  86.8 2.1 %collective-permute-start.4 = (bf16[768,16,128]{2,1,0:T(8,128)(2,1)S(1)}, bf16[768,16,128]{2,1,0:T(8,128)(2,1)S(1)}, u32[]{:S(2)}, u32[]{:S(2)}) collective-permute-start(bf16[768,16,128]{2,1,0:T(8,128)(2,1)S(1)} %together.1.own), channel_id=1, source_target_pairs={{0,8},{8,0},{1,9},{9,1},{2,10},{10,2},{3,11},{11,3},{4,12},{12,4},... | collective-permute-start | bytes 9437192 | tf_op jit(solution)/shard_map/ppermute | solution.py:372
  88.9 5.6 %collective-permute-done.4.swapped = bf16[768,16,128]{2,1,0:T(8,128)(2,1)S(1)} collective-permute-done((bf16[768,16,128]{2,1,0:T(8,128)(2,1)S(1)}, bf16[768,16,128]{2,1,0:T(8,128)(2,1)S(1)}, u32[]{:S(2)}, u32[]{:S(2)}) %collective-permute-start.4) | collective-permute-done | bytes 3145760 | tf_op jit(solution)/shard_map/ppermute | solution.py:372
  94.5 6.1 %precondition.1 = bf16[256,16,128]{2,1,0:T(8,128)(2,1)S(1)} custom-call(bf16[768,16,128]{2,1,0:T(8,128)(2,1)S(1)} %together.1.own, bf16[768,16,128]{2,1,0:T(8,128)(2,1)S(1)} %collective-permute-done.4.swapped), custom_call_target="tpu_custom_call" | custom-call | flops 4294967296 | bytes 10485760 | tf_op jit(solution)/shard_map/precondition/pallas_call | solution.py:312
  100.6 44.9 %all_to_all.10.returned = bf16[256,16,128]{2,1,0:T(8,128)(2,1)S(1)} all-to-all(bf16[256,16,128]{2,1,0:T(8,128)(2,1)S(1)} %precondition.1), channel_id=1, replica_groups=mesh['col'=32,'core'=2,'replica'=8] {'col','replica'}, dimensions={0} | all-to-all | bytes 2097152 | tf_op jit(solution)/shard_map/all_to_all | solution.py:368
  145.5 0.0 copy-done.1
  145.5 0.0 copy-done.2
  145.5 2.1 %finish.1 = bf16[16,16,8,128]{3,2,1,0:T(8,128)(2,1)} custom-call(s32[2,128]{1,0:T(2,128)S(1)} %copy-done.2, bf16[256,16,128]{2,1,0:T(8,128)(2,1)S(1)} %all_to_all.10.returned, bf16[16,16,8,128]{3,2,1,0:T(8,128)(2,1)S(1)} %copy-done.1), custom_call_target="tpu_custom_call" | custom-call | tf_op jit(solution)/shard_map/finish/pallas_call | solution.py:353
  (1 shorter events, 0.0 us)
Async XLA Ops:
  3.3 81.9 %collective-permute-start.1 = (bf16[16,128,128]{2,1,0:T(8,128)(2,1)}, bf16[16,128,128]{2,1,0:T(8,128)(2,1)}, u32[]{:S(2)}, u32[]{:S(2)}) collective-permute-start(bf16[16,128,128]{2,1,0:T(8,128)(2,1)} %get-tuple-element.16), channel_id=1, source_target_pairs={{3,2},{7,10},{4,3},{0,11},{5,4},{1,12},{15,14},{11,6},{8,15},{12,7... | collective-permute-start | bytes 1572872 | tf_op jit(solution)/shard_map/ppermute | solution.py:378
  14.8 70.4 %collective-permute-start.2 = (bf16[16,128,128]{2,1,0:T(8,128)(2,1)}, bf16[16,128,128]{2,1,0:T(8,128)(2,1)}, u32[]{:S(2)}, u32[]{:S(2)}) collective-permute-start(bf16[16,128,128]{2,1,0:T(8,128)(2,1)} %get-tuple-element.17), channel_id=1, source_target_pairs={{4,2},{0,10},{5,3},{1,11},{6,4},{2,12},{8,14},{12,6},{9,15},{13,7}... | collective-permute-start | bytes 1572872 | tf_op jit(solution)/shard_map/ppermute | solution.py:378
  16.7 68.5 %collective-permute-start = (bf16[16,128,128]{2,1,0:T(8,128)(2,1)}, bf16[16,128,128]{2,1,0:T(8,128)(2,1)}, u32[]{:S(2)}, u32[]{:S(2)}) collective-permute-start(bf16[16,128,128]{2,1,0:T(8,128)(2,1)} %get-tuple-element.13.after.own), channel_id=1, source_target_pairs={{6,10},{7,11},{0,12},{10,6},{11,7},{12,0},{22,26},{23,27},{16,28},... | collective-permute-start | bytes 1572872 | tf_op jit(solution)/shard_map/ppermute | solution.py:378
  18.2 67.0 %copy-start = (bf16[16,128,128]{2,1,0:T(8,128)(2,1)S(1)}, bf16[16,128,128]{2,1,0:T(8,128)(2,1)}, u32[]{:S(2)}) copy-start(bf16[16,128,128]{2,1,0:T(8,128)(2,1)} %get-tuple-element.13.after.own) | copy-start | bytes 1572868
  23.5 61.7 %collective-permute-start.3 = (bf16[16,128,128]{2,1,0:T(8,128)(2,1)}, bf16[16,128,128]{2,1,0:T(8,128)(2,1)S(1)}, u32[]{:S(2)}, u32[]{:S(2)}) collective-permute-start(bf16[16,128,128]{2,1,0:T(8,128)(2,1)} %released.1), channel_id=1, source_target_pairs={{5,2},{1,10},{6,3},{2,11},{7,4},{3,12},{9,14},{13,6},{10,15},{14,7... | collective-permute-start | bytes 1572872 | tf_op jit(solution)/shard_map/ppermute | solution.py:381
  86.8 58.7 %copy-start.1 = (bf16[16,16,8,128]{3,2,1,0:T(8,128)(2,1)S(1)}, bf16[16,16,8,128]{3,2,1,0:T(8,128)(2,1)}, u32[]{:S(2)}) copy-start(bf16[16,16,8,128]{3,2,1,0:T(8,128)(2,1)} %momentum.1) | copy-start | bytes 1572868
  86.8 58.7 %copy-start.2 = (s32[2,128]{1,0:T(2,128)S(1)}, s32[2,128]{1,0:T(2,128)}, u32[]{:S(2)}) copy-start(s32[2,128]{1,0:T(2,128)} %get-tuple-element.14.place) | copy-start | bytes 3076
  86.8 7.7 %collective-permute-start.4 = (bf16[768,16,128]{2,1,0:T(8,128)(2,1)S(1)}, bf16[768,16,128]{2,1,0:T(8,128)(2,1)S(1)}, u32[]{:S(2)}, u32[]{:S(2)}) collective-permute-start(bf16[768,16,128]{2,1,0:T(8,128)(2,1)S(1)} %together.1.own), channel_id=1, source_target_pairs={{0,8},{8,0},{1,9},{9,1},{2,10},{10,2},{3,11},{11,3},{4,12},{12,4},... | collective-permute-start | bytes 9437192 | tf_op jit(solution)/shard_map/ppermute | solution.py:372
